TPU v7x, 128 devices: a whole 4x4x4 slice. The times are simulated.
128 devices in a mesh: lon: 16 (over z_hi, x, core), lat: 8 (over y, z_lo).
Axes of the slice: x: 4, y: 4, z: 4 (z_hi: 2, z_lo: 2; z = z_hi * 2 + z_lo), core: 2. Of those that a mesh axis runs over, the one named last changes fastest.
Arguments:
- tokens: bfloat16 [1024, 256, 512], P('lon', 'lat'), may hold values from -6 to 6
- pad_mask: int32 [1024, 256], replicated, may hold values 0 or 1
- shifts: int32 [2], replicated, may hold values from 1 to 7
- bias_table: float32 [8, 225], replicated, may hold values from -4 to 4
- rel_index: int32 [64, 64], replicated, may hold values from 0 to 224
- w_qkv: bfloat16 [512, 1536], replicated, may hold values from -0.25 to 0.25
- w_out: bfloat16 [512, 512], replicated, may hold values from -0.25 to 0.25
- grad_out: bfloat16 [1024, 256, 512], P('lon', 'lat'), may hold values from -6 to 6
Outputs:
- updated: bfloat16 [1024, 256, 512], P('lon', 'lat')
- tokens_grad: bfloat16 [1024, 256, 512], P('lon', 'lat')
- qkv_weight_grad: float32 [512, 1536], P(('lon', 'lat'))
- out_weight_grad: float32 [512, 512], P(('lon', 'lat'))
All inputs are finite; a program needn't handle non-finite values.
Results may differ from a plain program's by a relative error of at most 0.009.
Values may be sent and summed in bfloat16 or wider, within the bound.
No kernel may reach another device: no remote copies, remote signals or barrier semaphores. Data moves between devices by JAX's collectives and lax.ppermute only.
A program may use at most 128 MiB of HBM per device.

v0:
```python
import jax
import jax.numpy as jnp
from jax import lax
from jax.experimental import pallas as pl
from jax.experimental.pallas import tpu as pltpu
from jax.sharding import Mesh, PartitionSpec as P

WIN = 8
CELLS = 64
D = 512
HEADS = 8
GROUP = 256
BF = jnp.bfloat16
F32 = jnp.float32
LOG2E = 1.4426950408889634
SCALE = 0.125
VMEM_LIMIT = 56 * 2**20
LON = ("zh", "x", "core")
LAT = ("y", "zl")
ALL = LON + LAT


def dot_nn(a, b):
    return lax.dot_general(a, b, (((1,), (0,)), ((), ())), preferred_element_type=F32)


def dot_nt(a, b):
    return lax.dot_general(a, b, (((1,), (1,)), ((), ())), preferred_element_type=F32)


def dot_tn(a, b):
    return lax.dot_general(a, b, (((0,), (0,)), ((), ())), preferred_element_type=F32)


def iota(shape, dim):
    return lax.broadcasted_iota(jnp.int32, shape, dim)


def keep_window(x, g, row, xt, xg, hid, istd):
    at = pl.ds(row, CELLS)
    center = x - jnp.mean(x, axis=-1, keepdims=True)
    inv = lax.rsqrt(jnp.mean(center * center, axis=-1, keepdims=True) + 1e-05)
    hid[at, :] = (center * inv).astype(BF)
    istd[at, :] = jnp.broadcast_to(inv, (CELLS, 128))
    xt[at, :] = x.astype(BF)
    xg[at, :] = g.astype(BF)


def project_rows(first, count, hid, xg, w_qkv, w_out, qkvg):
    at = pl.ds(first, count)
    qkvg[at, : 3 * D] = dot_nn(hid[at, :], w_qkv[...]).astype(BF)
    qkvg[at, 3 * D :] = dot_nt(xg[at, :], w_out[...]).astype(BF)


def project(rows, chunk, hid, xg, w_qkv, w_out, qkvg):
    def step(c, carry):
        project_rows(pl.multiple_of(c * chunk, 64), chunk, hid, xg, w_qkv, w_out, qkvg)
        return carry

    lax.fori_loop(0, rows // chunk, step, 0)


def fill_ones(ones):
    block = (iota((GROUP, GROUP), 0) >> 6) == (iota((GROUP, GROUP), 1) >> 6)
    ones[...] = jnp.where(block, 1.0, 0.0).astype(BF)


def attend(first, marks, thrs, bias, ones, qkvg, mix, dq):
    lane = iota((CELLS, 128), 1)
    cell = iota((CELLS, 128), 0)
    diag = (lane & 63) == cell
    low_half = lane < 64
    low_mask = jnp.where(low_half, 1.0, 0.0).astype(BF)
    high_mask = jnp.where(low_half, 0.0, 1.0).astype(BF)
    zero = jnp.zeros((CELLS, 128), BF)

    def by_head(x):
        a, b = x[:, :128], x[:, 128:]
        rows = [(a * low_mask, zero), (a * high_mask, zero), (zero, b * low_mask), (zero, b * high_mask)]
        return jnp.concatenate([jnp.concatenate(r, axis=1) for r in rows], axis=0)

    units = []
    for w, (mark, thr) in enumerate(zip(marks, thrs)):
        row = pl.multiple_of((first + w) * CELLS, CELLS)
        same = ((lane & 7) >= thr) == ((cell & 7) >= thr)
        valid = jnp.broadcast_to(mark, (CELLS, 128)) > 0.5
        ok = (valid & same) | diag
        ok = jnp.concatenate([ok, ok], axis=1)
        for h in range(2):
            c = h * GROUP
            at = pl.ds(row, CELLS)
            q = qkvg[at, c : c + GROUP]
            k = qkvg[at, D + c : D + c + GROUP]
            v = qkvg[at, 2 * D + c : 2 * D + c + GROUP]
            g = qkvg[at, 3 * D + c : 3 * D + c + GROUP]
            kbd, vbd = by_head(k), by_head(v)
            s = dot_nt(q, kbd)
            pg = dot_nt(g, vbd)
            e = jnp.where(ok, jnp.exp2(s * (SCALE * LOG2E) + bias[:, c : c + GROUP]), 0.0)
            units.append((at, c, q, g, kbd, vbd, e, pg))
    total = dot_nn(jnp.concatenate([u[6].astype(BF) for u in units], axis=0), ones[...])
    probs = []
    for n, u in enumerate(units):
        probs.append(u[6] / total[n * CELLS : (n + 1) * CELLS])
    dots = dot_nn(
        jnp.concatenate([(p * u[7]).astype(BF) for p, u in zip(probs, units)], axis=0), ones[...]
    )
    for n, (at, c, q, g, kbd, vbd, e, pg) in enumerate(units):
        p = probs[n]
        p_low = p.astype(BF)
        ds = (p * (pg - dots[n * CELLS : (n + 1) * CELLS]) * SCALE).astype(BF)
        mix[at, c : c + GROUP] = dot_nn(p_low, vbd).astype(BF)
        dq[at, c : c + GROUP] = dot_nn(ds, kbd).astype(BF)
        for t in range(2):
            lo, hi = t * 128, t * 128 + 128
            kg = dot_tn(ds[:, lo:hi], q[:, lo:hi])
            vg = dot_tn(p_low[:, lo:hi], g[:, lo:hi])
            dq[at, D + c + lo : D + c + hi] = jnp.where(low_half, kg[:64], kg[64:]).astype(BF)
            dq[at, 2 * D + c + lo : 2 * D + c + hi] = jnp.where(low_half, vg[:64], vg[64:]).astype(BF)


def finish(at, xt, xg, hid, istd, mix, dq, w_qkv, w_out):
    update = xt[at, :].astype(F32) + dot_nn(mix[at, :], w_out[...])
    normed_grad = dot_nt(dq[at, :], w_qkv[...])
    normed = hid[at, :].astype(F32)
    centred = normed_grad - jnp.mean(normed_grad, axis=-1, keepdims=True)
    centred = centred - normed * jnp.mean(normed_grad * normed, axis=-1, keepdims=True)
    inv = istd[at, :]
    return update, xg[at, :].astype(F32) + jnp.concatenate([inv] * 4, axis=1) * centred


def rows_of(strip):
    return strip.reshape(CELLS, D)


def strip_of(rows, count):
    parts = [rows[n * CELLS : (n + 1) * CELLS].reshape(WIN, WIN, D) for n in range(count)]
    return jnp.concatenate(parts + [jnp.zeros((WIN, WIN, D), F32)], axis=1)


def make_tables(marks_in, bias_table, rel_index, s0, s1, keys, bias, table, rel):
    rows = pltpu.roll(marks_in[...].astype(F32), 72 - s0, 0)[:64]
    lane = iota((256, 512), 1)
    place = (lax.axis_index(LAT) * 32 + s1 + (lane >> 7) * 8 + (lane & 7)) & 255
    pick = jnp.where(iota((256, 512), 0) == place, 1.0, 0.0).astype(BF)
    marks = dot_nn(rows.astype(BF), pick)
    own = (iota((64, 512), 0) & 7) == ((iota((64, 512), 1) & 63) >> 3)
    marks = jnp.sum(jnp.where(own, marks, 0.0).reshape(8, 8, 512), axis=1)
    for b in range(4):
        keys[8 * b : 8 * b + 8, :] = marks[:, 128 * b : 128 * b + 128]

    table[...] = jnp.zeros((8, 256), F32)
    table[:, :225] = bias_table[...] * LOG2E
    rel[:, :64] = rel_index[...]
    rel[:, 64:] = rel_index[...]
    at = rel[...]
    low = at < 128
    at = at & 127
    left = iota((CELLS, 128), 1) < 64
    for pair in range(4):
        found = []
        for h in (2 * pair, 2 * pair + 1):
            half = [
                jnp.take_along_axis(
                    jnp.broadcast_to(table[h : h + 1, c : c + 128], (CELLS, 128)), at, axis=1
                )
                for c in (0, 128)
            ]
            found.append(jnp.where(low, half[0], half[1]))
        bias[:, pair * 128 : pair * 128 + 128] = jnp.where(left, found[0], found[1])


def start_all(pairs, sems, first=0):
    copies = [pltpu.make_async_copy(a, b, sems.at[first + n]) for n, (a, b) in enumerate(pairs)]
    for copy in copies:
        copy.start()
    return copies


def wait_all(copies):
    for copy in copies:
        copy.wait()


def interior_kernel(
    shifts, tokens_in, grads_in, pad_in, bias_table, rel_index, w_qkv_in, w_out_in,
    updated_out, grad_out, w_part, keys, bias,
    tokens, grads, w_qkv, w_out, marks, updated, tokens_grad,
    xt, xg, hid, istd, qkvg, mix, dq, ones, table, rel, w_sum, sems,
):
    s0, s1 = shifts[0], shifts[1]
    base = lax.axis_index(LON) * 64
    mark_copies = start_all(
        [
            (pad_in.at[pl.ds(pl.multiple_of(base, 8), 64)], marks.at[0:64]),
            (pad_in.at[pl.ds(pl.multiple_of((base + 64) & 1023, 8), 8)], marks.at[64:72]),
        ],
        sems,
    )
    rows_in = start_all([(tokens_in, tokens), (grads_in, grads)], sems, 2)
    weights_in = start_all([(w_qkv_in, w_qkv), (w_out_in, w_out)], sems, 4)
    fill_ones(ones)
    wait_all(mark_copies)
    make_tables(marks, bias_table, rel_index, s0, s1, keys, bias, table, rel)
    wait_all(rows_in)

    def load(a, carry):
        at = pl.ds(s0 + a * WIN, WIN)
        x = pltpu.roll(tokens[at, :, :].astype(F32), 32 - s1, 1)
        g = pltpu.roll(grads[at, :, :].astype(F32), 32 - s1, 1)
        for b in range(3):
            row = pl.multiple_of((a * 3 + b) * CELLS, CELLS)
            c = slice(b * WIN, b * WIN + WIN)
            keep_window(rows_of(x[:, c]), rows_of(g[:, c]), row, xt, xg, hid, istd)
        return carry

    lax.fori_loop(0, 7, load, 0)
    wait_all(weights_in)
    project(21 * CELLS, 448, hid, xg, w_qkv, w_out, qkvg)

    def windows(a):
        seen = [keys[pl.ds(8 * b + a, 1), :] for b in range(3)]
        attend(a * 3, seen, [8] * 3, bias, ones, qkvg, mix, dq)

    def store(a):
        at = pl.ds(pl.multiple_of(a * 192, 64), 192)
        to = pl.ds(s0 + a * WIN, WIN)
        for rows, out in zip(finish(at, xt, xg, hid, istd, mix, dq, w_qkv, w_out), (updated, tokens_grad)):
            out[to, :, :] = pltpu.roll(strip_of(rows, 3), s1, 1).astype(BF)

    def step(a, carry):
        store(a - 1)
        windows(a)
        return carry

    windows(0)
    lax.fori_loop(1, 7, step, 0)
    store(6)
    copies = start_all([(updated, updated_out), (tokens_grad, grad_out)], sems, 2)
    for b in range(2):
        r = slice(b * 256, (b + 1) * 256)
        w_sum[r, : 3 * D] = dot_tn(hid[:, r], dq[...])
        w_sum[r, 3 * D :] = dot_tn(mix[:, r], xg[...])
        copies += start_all([(w_sum.at[r], w_part.at[r])], sems, b)
    wait_all(copies)


def edge_kernel(
    shifts, tokens_in, grads_in, halo_lon, halo_lat, halo_cor, keys, bias, w_qkv_in, w_out_in, w_part,
    lat_up, lon_up, lat_grad, lon_grad, out_lat, out_lon, w_mine, w_other,
    tok, grad, far, low_tok, low_grad, low_far, w_qkv, w_out, to_lat, to_lon,
    xt, xg, hid, istd, qkvg, mix, dq, ones, w_sum, sems,
):
    s0, s1 = shifts[0], shifts[1]
    core = lax.axis_index("core")
    thr_edge = jnp.where(lax.axis_index(LAT) == 7, 8 - s1, 8)
    rows_in = start_all(
        [
            (tokens_in.at[:, 16:32, :], tok),
            (grads_in.at[:, 16:32, :], grad),
            (halo_lat, far),
            (tokens_in.at[56:64], low_tok.at[0:8]),
            (grads_in.at[56:64], low_grad.at[0:8]),
            (halo_lon.at[:, :, 0:D], low_tok.at[8:16]),
            (halo_lon.at[:, :, D : 2 * D], low_grad.at[8:16]),
            (halo_lat.at[56:64], low_far.at[0:8]),
            (halo_cor, low_far.at[8:16]),
        ],
        sems,
    )
    weights_in = start_all([(w_qkv_in, w_qkv), (w_out_in, w_out), (w_part, w_sum)], sems, 9)
    fill_ones(ones)
    tail = slice(11 * CELLS, 12 * CELLS)
    xg[tail, :] = jnp.zeros((CELLS, D), BF)
    hid[tail, :] = jnp.zeros((CELLS, D), BF)
    wait_all(rows_in)

    def load(a, carry):
        at = pl.ds(s0 + a * WIN, WIN)
        found = []
        for near, c in ((tok, 0), (grad, D)):
            rows = [near[at, 8:16, :].astype(F32), far[at, :, c : c + D].astype(F32)]
            found.append(rows_of(pltpu.roll(jnp.concatenate(rows, axis=1), 16 - s1, 1)[:, :8]))
        keep_window(*found, pl.multiple_of(a * CELLS, CELLS), xt, xg, hid, istd)
        return carry

    lax.fori_loop(0, 7, load, 0)
    at = pl.ds(s0, WIN)
    found = []
    for near, c in ((low_tok, 0), (low_grad, D)):
        rows = [near[at, :, :].astype(F32), low_far[at, :, c : c + D].astype(F32)]
        found.append(pltpu.roll(jnp.concatenate(rows, axis=1), 40 - s1, 1))
    for b in range(4):
        x, g = (rows_of(rows[:, b * WIN : b * WIN + WIN]) for rows in found)
        keep_window(x, g, (7 + b) * CELLS, xt, xg, hid, istd)
    wait_all(weights_in)
    project(12 * CELLS, 384, hid, xg, w_qkv, w_out, qkvg)

    def windows(a, carry):
        seen, thr = [], []
        for w in range(3):
            n = a * 3 + w
            row = jnp.where(n < 7, 24 + n, jnp.minimum(8 * n - 49, 31))
            seen.append(keys[pl.ds(row, 1), :])
            thr.append(jnp.where((n < 7) | (n == 10), thr_edge, 8))
        attend(a * 3, seen, thr, bias, ones, qkvg, mix, dq)
        return carry

    lax.fori_loop(0, 4, windows, 0)

    results = finish(slice(0, 7 * CELLS), xt, xg, hid, istd, mix, dq, w_qkv, w_out)
    for rows, near, c in zip(results, (tok, grad), (0, D)):
        for a in range(7):
            strip = strip_of(rows[a * CELLS : (a + 1) * CELLS], 1)
            strip = pltpu.roll(strip, s1, 1).astype(BF)
            near[pl.ds(s0 + a * WIN, WIN), 0:8, :] = strip[:, :8]
            to_lat[pl.ds(s0 + a * WIN, WIN), :, c : c + D] = strip[:, 8:]
    results = finish(slice(7 * CELLS, 11 * CELLS), xt, xg, hid, istd, mix, dq, w_qkv, w_out)
    for rows, low, c in zip(results, (low_tok, low_grad), (0, D)):
        strip = pltpu.roll(strip_of(rows, 4), s1, 1).astype(BF)
        low[pl.ds(s0, WIN), :, :] = strip[:, :32]
        to_lat[pl.ds(s0 + 56, WIN), :, c : c + D] = strip[:, 32:]
    to_lon[:, :, 0:D] = low_tok[8:16]
    to_lon[:, :, D : 2 * D] = low_grad[8:16]
    copies = start_all(
        [
            (tok, lat_up),
            (grad, lat_grad),
            (low_tok.at[0:8], lon_up),
            (low_grad.at[0:8], lon_grad),
            (to_lat, out_lat),
            (to_lon, out_lon),
        ],
        sems,
    )
    for b in range(2):
        r = slice(b * 256, (b + 1) * 256)
        w_sum[r, : 3 * D] += dot_tn(hid[:, r], dq[...])
        w_sum[r, 3 * D :] += dot_tn(mix[:, r], xg[...])

    def split(n, carry):
        to = pl.ds(pl.multiple_of(n * 32, 32), 32)
        w_mine[to, :] = w_sum[pl.ds(pl.multiple_of((2 * n + core) * 32, 32), 32), :].astype(BF)
        w_other[to, :] = w_sum[pl.ds(pl.multiple_of((2 * n + 1 - core) * 32, 32), 32), :].astype(BF)
        return carry

    lax.fori_loop(0, 8, split, 0)
    wait_all(copies)


def edge_merge_kernel(
    shifts, updated, tokens_grad, lat_up, lon_up, lat_grad, lon_grad, out_updated, out_grad,
    side, low, sems,
):
    s0, s1 = shifts[0], shifts[1]
    pairs = []
    for n, out in enumerate((out_updated, out_grad)):
        pairs += [(out.at[:, 16:32, :], side.at[n]), (out.at[56:64, 0:16, :], low.at[n])]
    wait_all(start_all(pairs, sems))
    mark = iota((8, 8, D), 1) >= s1
    for n, (lat, lon) in enumerate(((lat_up, lon_up), (lat_grad, lon_grad))):

        def rest(r, carry, n=n, lat=lat):
            at = pl.ds(pl.multiple_of(r * 8, 8), 8)
            rows = side[n, at, 8:16, :].astype(F32)
            side[n, at, 8:16, :] = jnp.where(mark, lat[at, 0:8, :].astype(F32), rows).astype(BF)
            return carry

        lax.fori_loop(0, 8, rest, 0)
        later = iota((8, 16, D), 0) >= s0
        rows = side[n, 56:64, :, :].astype(F32)
        side[n, 56:64, :, :] = jnp.where(later, lon[:, 16:32, :].astype(F32), rows).astype(BF)
        later = later & (iota((8, 16, D), 1) >= s1)
        rows = low[n].astype(F32)
        low[n] = jnp.where(later, lon[:, 0:16, :].astype(F32), rows).astype(BF)
    wait_all(start_all([(b, a) for a, b in pairs], sems))


def lat_return_kernel(
    shifts, updated, tokens_grad, in_lat, out_lon, out_updated, out_grad, to_lon, side, sems
):
    s1 = shifts[1]
    pairs = [(out.at[:, 0:16, :], side.at[n]) for n, out in enumerate((out_updated, out_grad))]
    copies = start_all(pairs, sems)
    mark = iota((8, 8, D), 1) < s1
    for n in range(2):
        cols = slice(n * D, n * D + D)
        first = jnp.where(mark, in_lat[64:72, :, cols].astype(F32), out_lon[:, 0:8, cols].astype(F32))
        to_lon[:, 0:8, cols] = first.astype(BF)
        to_lon[:, 8:32, cols] = out_lon[:, 8:32, cols]
    wait_all(copies)
    for n in range(2):

        def place(r, carry, n=n):
            at = pl.ds(pl.multiple_of(r * 8, 8), 8)
            rows = side[n, at, 0:8, :].astype(F32)
            came = in_lat[at, :, n * D : n * D + D].astype(F32)
            side[n, at, 0:8, :] = jnp.where(mark, came, rows).astype(BF)
            return carry

        lax.fori_loop(0, 8, place, 0)
    wait_all(start_all([(b, a) for a, b in pairs], sems))


def lon_return_kernel(shifts, updated, tokens_grad, in_lon, out_updated, out_grad, top, sems):
    s0 = shifts[0]
    pairs = [(out.at[0:8], top.at[n]) for n, out in enumerate((out_updated, out_grad))]
    wait_all(start_all(pairs, sems))
    early = iota((8, 32, D), 0) < s0
    for n in range(2):
        came = in_lon[:, :, n * D : n * D + D].astype(F32)
        top[n] = jnp.where(early, came, top[n].astype(F32)).astype(BF)
    wait_all(start_all([(b, a) for a, b in pairs], sems))


def vmem(shape, dtype):
    return pltpu.VMEM(shape, dtype)


def sds(shape, dtype):
    return jax.ShapeDtypeStruct(shape, dtype)


IN_VMEM = pl.BlockSpec(memory_space=pltpu.VMEM)
IN_SMEM = pl.BlockSpec(memory_space=pltpu.SMEM)
IN_HBM = pl.BlockSpec(memory_space=pl.ANY)


def call(kernel, out_shape, scratch, in_specs, out_specs, aliases=None):
    return pl.pallas_call(
        kernel,
        out_shape=out_shape,
        in_specs=[IN_SMEM] + in_specs,
        out_specs=out_specs,
        scratch_shapes=scratch,
        input_output_aliases=aliases or {},
        compiler_params=pltpu.CompilerParams(vmem_limit_bytes=VMEM_LIMIT),
    )


def window_scratch(rows):
    return [vmem((rows, D), BF), vmem((rows, D), BF), vmem((rows, D), BF), vmem((rows, 128), F32)]


def attend_scratch(rows):
    return [
        vmem((rows, 4 * D), BF),
        vmem((rows, D), BF),
        vmem((rows, 3 * D), BF),
        vmem((GROUP, GROUP), BF),
    ]


def shift_to(value, d_lon, d_lat):
    pairs = []
    for a in range(16):
        for b in range(8):
            pairs.append((a * 8 + b, ((a + d_lon) % 16) * 8 + (b + d_lat) % 8))
    return lax.ppermute(value, ALL, pairs)


def scatter_sum(blocks, axes, count, beside=None):
    here = lax.axis_index(axes)
    parts = [lax.dynamic_index_in_dim(blocks, here, 0, keepdims=False)]
    for step in range(1, count):
        block = lax.dynamic_index_in_dim(blocks, (here + step) % count, 0, keepdims=False)
        pairs = [(n, (n + step) % count) for n in range(count)]
        parts.append(lax.ppermute(block, axes, pairs))
    extra = None
    if beside is not None:
        extra = beside(blocks)
        parts, extra = lax.optimization_barrier((parts, extra))
    total = parts[0].astype(F32)
    for part in parts[1:]:
        total = total + part.astype(F32)
    return total, extra


INNER, OUTER = 21 * CELLS, 12 * CELLS
GRID = sds((64, 32, D), BF)
DMA = pltpu.SemaphoreType.DMA


WEIGHTS = [vmem((D, 3 * D), BF), vmem((D, D), BF)]


def run_interior(*args):
    rows = vmem((64, 32, D), BF)
    return call(
        interior_kernel,
        [GRID, GRID, sds((D, 4 * D), F32), sds((32, 128), F32), sds((64, 512), F32)],
        [rows, rows, *WEIGHTS, vmem((72, 256), jnp.int32), rows, rows]
        + window_scratch(INNER)
        + attend_scratch(INNER)
        + [vmem((8, 256), F32), vmem((64, 128), jnp.int32), vmem((D, 4 * D), F32), DMA((6,))],
        [IN_HBM] * 3 + [IN_VMEM] * 2 + [IN_HBM] * 2,
        [IN_HBM] * 3 + [IN_VMEM] * 2,
    )(*args)


def run_edge(*args):
    lat, lon = (64, 16, D), (8, 32, D)
    far_lat, far_lon = (64, 8, 2 * D), (8, 32, 2 * D)
    return call(
        edge_kernel,
        [sds(shape, BF) for shape in (lat, lon, lat, lon, (72, 8, 2 * D), far_lon)]
        + [sds((D // 2, 4 * D), BF)] * 2,
        [vmem(lat, BF), vmem(lat, BF), vmem(far_lat, BF)]
        + [vmem((16, 32, D), BF), vmem((16, 32, D), BF), vmem((16, 8, 2 * D), BF)]
        + WEIGHTS
        + [vmem((72, 8, 2 * D), BF), vmem(far_lon, BF)]
        + window_scratch(OUTER)
        + attend_scratch(OUTER)
        + [vmem((D, 4 * D), F32), DMA((12,))],
        [IN_HBM] * 5 + [IN_VMEM] * 2 + [IN_HBM] * 3,
        [IN_HBM] * 6 + [IN_VMEM] * 2,
    )(*args)


def run_edge_merge(*args):
    return call(
        edge_merge_kernel,
        [GRID, GRID],
        [vmem((2, 64, 16, D), BF), vmem((2, 8, 16, D), BF), DMA((4,))],
        [IN_HBM] * 2 + [IN_VMEM] * 4,
        [IN_HBM] * 2,
        {1: 0, 2: 1},
    )(*args)


def run_lat_return(*args):
    return call(
        lat_return_kernel,
        [GRID, GRID, sds((8, 32, 2 * D), BF)],
        [vmem((2, 64, 16, D), BF), DMA((2,))],
        [IN_HBM] * 2 + [IN_VMEM] * 2,
        [IN_HBM] * 2 + [IN_VMEM],
        {1: 0, 2: 1},
    )(*args)


def run_lon_return(*args):
    return call(
        lon_return_kernel,
        [GRID, GRID],
        [vmem((2, 8, 32, D), BF), DMA((2,))],
        [IN_HBM] * 2 + [IN_VMEM],
        [IN_HBM] * 2,
        {1: 0, 2: 1},
    )(*args)


def local(tokens, pad_mask, shifts, bias_table, rel_index, w_qkv, w_out, grad_out):
    both = lambda a, b: jnp.concatenate([tokens[a, b], grad_out[a, b]], axis=-1)
    halo_lat = shift_to(both(slice(None), slice(0, 8)), 0, -1)
    halo_lon = shift_to(both(slice(0, 8), slice(None)), -1, 0)
    halo_cor = shift_to(both(slice(0, 8), slice(0, 8)), -1, -1)

    updated, tokens_grad, w_part, keys, bias = run_interior(
        shifts, tokens, grad_out, pad_mask, bias_table, rel_index, w_qkv, w_out
    )
    *edges, out_lat, out_lon, w_mine, w_other = run_edge(
        shifts, tokens, grad_out, halo_lon, halo_lat, halo_cor, keys, bias, w_qkv, w_out, w_part
    )

    def merge_beside(blocks):
        _, *placed = lax.optimization_barrier((blocks, updated, tokens_grad))
        return run_edge_merge(shifts, *placed, *edges)

    in_lat = shift_to(out_lat, 0, 1)
    w_got = lax.ppermute(w_other, "core", [(0, 1), (1, 0)])
    total = (w_mine.astype(F32) + w_got.astype(F32)).astype(BF)
    total = total.reshape(2, 4, 32, 4 * D).transpose(1, 0, 2, 3)
    total, (updated, tokens_grad) = scatter_sum(total, "x", 4, merge_beside)
    total = total.astype(BF).reshape(2, 4, 8, 4 * D).transpose(1, 0, 2, 3)
    lat_beside = lambda blocks: run_lat_return(shifts, updated, tokens_grad, in_lat, out_lon)
    total, (updated, tokens_grad, out_lon) = scatter_sum(total, "y", 4, lat_beside)
    in_lon = shift_to(out_lon, 1, 0)
    total, _ = scatter_sum(total.astype(BF).reshape(4, 4, 4 * D), ("zh", "zl"), 4)

    updated, tokens_grad = run_lon_return(shifts, updated, tokens_grad, in_lon)
    return (updated, tokens_grad, total[:, : 3 * D], total[:, 3 * D :])


def solution(mesh):
    fine = Mesh(mesh.devices.reshape(2, 4, 2, 4, 2), ALL)
    in_specs = (P(LON, LAT, None), P(), P(), P(), P(), P(), P(), P(LON, LAT, None))
    out_specs = (P(LON, LAT, None), P(LON, LAT, None), P(ALL, None), P(ALL, None))
    return jax.shard_map(local, mesh=fine, in_specs=in_specs, out_specs=out_specs, check_vma=False)
```

profile of v0, /device:TPU:0, one launch (start us, length us, event | category | flops | bytes accessed | tf_op | source)
XLA Modules:
  0.0 116.6 jit_solution(16575045694563860075)
XLA Ops:
  0.7 1.0 slice-done.2
  1.7 0.2 slice-done
  1.8 0.1 pad_maximum_fusion
  2.0 4.5 %collective-permute-start.1 = (bf16[64,8,1024]{2,1,0:T(8,128)(2,1)S(1)}, bf16[64,8,1024]{2,1,0:T(8,128)(2,1)S(1)}, u32[]{:S(2)}, u32[]{:S(2)}) collective-permute-start(bf16[64,8,1024]{2,1,0:T(8,128)(2,1)S(1)} %pad_maximum_fusion), channel_id=1, source_target_pairs={{0,7},{1,0},{2,1},{3,2},{4,3},{5,4},{6,5},{7,6},{8,15},{9,8},{10,9... | collective-permute-start | bytes 3145736 | tf_op jit(solution)/shard_map/ppermute | solution.py:459
  6.6 5.0 %collective-permute-start = (bf16[8,32,1024]{2,1,0:T(8,128)(2,1)S(1)}, bf16[8,32,1024]{2,1,0:T(8,128)(2,1)S(1)}, u32[]{:S(2)}, u32[]{:S(2)}) collective-permute-start(bf16[8,32,1024]{2,1,0:T(8,128)(2,1)S(1)} %pad_maximum_fusion.1), channel_id=1, source_target_pairs={{0,120},{1,121},{2,122},{3,123},{4,124},{5,125},{6,126},{7,127},{8... | collective-permute-start | bytes 1572872 | tf_op jit(solution)/shard_map/ppermute | solution.py:459
  11.6 0.3 collective-permute-start.2
  11.9 29.4 %shard_map.111 = (bf16[64,32,512]{2,1,0:T(8,128)(2,1)}, bf16[64,32,512]{2,1,0:T(8,128)(2,1)}, f32[512,2048]{1,0:T(8,128)}, f32[32,128]{1,0:T(8,128)}, f32[64,512]{1,0:T(8,128)}) custom-call(s32[2]{0:T(128)} %shifts.9, bf16[64,32,512]{2,1,0:T(8,128)(2,1)} %tokens_in.3, bf16[64,32,512]{2,1,0:T(8,128)(2,1)} %grads_in.3, s32[1024,256]{1,0:T(8,128)} %pad_in.1, ...), custom_call_target="tpu_custom_call" | custom-call | tf_op jit(solution)/shard_map/pallas_call | solution.py:489
  41.4 0.6 copy-done.6
  42.0 0.2 copy-done.5
  42.2 0.4 copy-done.3
  42.5 18.4 %shard_map.112 = (bf16[64,16,512]{2,1,0:T(8,128)(2,1)}, bf16[8,32,512]{2,1,0:T(8,128)(2,1)}, bf16[64,16,512]{2,1,0:T(8,128)(2,1)}, bf16[8,32,512]{2,1,0:T(8,128)...) custom-call(s32[2]{0:T(128)} %shifts.9, ...), custom_call_target="tpu_custom_call" | custom-call | tf_op jit(solution)/shard_map/pallas_call | solution.py:504
  61.0 1.9 %collective-permute-start.10 = (bf16[72,8,1024]{2,1,0:T(8,128)(2,1)}, bf16[72,8,1024]{2,1,0:T(8,128)(2,1)S(1)}, u32[]{:S(2)}, u32[]{:S(2)}) collective-permute-start(bf16[72,8,1024]{2,1,0:T(8,128)(2,1)} %get-tuple-element.60), channel_id=1, source_target_pairs={{0,1},{1,2},{2,3},{3,4},{4,5},{5,6},{6,7},{7,0},{8,9},{9,10},{10,1... | collective-permute-start | bytes 3538952 | tf_op jit(solution)/shard_map/ppermute | solution.py:459
  62.9 0.9 collective-permute-done.3
  63.8 1.6 %add_convert_fusion = bf16[256,2048]{1,0:T(8,128)(2,1)S(1)} fusion(bf16[256,2048]{1,0:T(8,128)(2,1)S(1)} %collective-permute-done.3, bf16[256,2048]{1,0:T(8,128)(2,1)} %get-tuple-element.42), kind=kLoop, calls=%fused_computation | loop fusion | flops 2097152 | bytes 3145728 | tf_op jit(solution)/shard_map/convert_element_type | solution.py:572
  65.7 0.2 collective-permute-start.5
  65.9 3.0 %collective-permute-start.6 = (bf16[2,32,2048]{2,1,0:T(8,128)(2,1)S(1)}, bf16[2,32,2048]{2,1,0:T(8,128)(2,1)S(1)}, u32[]{:S(2)}, u32[]{:S(2)}) collective-permute-start(bf16[2,32,2048]{2,1,0:T(8,128)(2,1)S(1)} %get-tuple-element.74), channel_id=1, source_target_pairs={{0,48},{16,0},{32,16},{48,32},{1,49},{17,1},{33,17},{49,33},{2,50}... | collective-permute-start | bytes 786440 | tf_op jit(solution)/shard_map/ppermute | solution.py:468
  68.9 5.1 %shard_map.113 = (bf16[64,32,512]{2,1,0:T(8,128)(2,1)}, bf16[64,32,512]{2,1,0:T(8,128)(2,1)}) custom-call(s32[2]{0:T(128)} %shifts.9, bf16[64,32,512]{2,1,0:T(8,128)(2,1)} %get-tuple-element.46.updated, bf16[64,32,512]{2,1,0:T(8,128)(2,1)} %get-tuple-element.47.tokens_grad, ...), custom_call_target="tpu_custom_call", output_to_operand_aliasing={{0}: (1, {}), {1}: (2, {})} | custom-call | tf_op jit(solution)/shard_map/pallas_call | solution.py:521
  73.9 6.9 %collective-permute-done.4 = bf16[2,32,2048]{2,1,0:T(8,128)(2,1)S(1)} collective-permute-done((bf16[2,32,2048]{2,1,0:T(8,128)(2,1)S(1)}, bf16[2,32,2048]{2,1,0:T(8,128)(2,1)S(1)}, u32[]{:S(2)}, u32[]{:S(2)}) %collective-permute-start.4) | collective-permute-done | bytes 262176 | tf_op jit(solution)/shard_map/ppermute | solution.py:468
  80.8 0.6 collective-permute-done.6
  81.7 2.2 %collective-permute-start.8 = (bf16[2,8,2048]{2,1,0:T(8,128)(2,1)S(1)}, bf16[2,8,2048]{2,1,0:T(8,128)(2,1)S(1)}, u32[]{:S(2)}, u32[]{:S(2)}) collective-permute-start(bf16[2,8,2048]{2,1,0:T(8,128)(2,1)S(1)} %get-tuple-element.79), channel_id=1, source_target_pairs={{0,4},{2,6},{4,0},{6,2},{1,5},{3,7},{5,1},{7,3},{8,12},{10,14},{12... | collective-permute-start | bytes 196616 | tf_op jit(solution)/shard_map/ppermute | solution.py:468
  83.9 1.1 collective-permute-start.9
  85.0 8.7 %collective-permute-done.10.in_lat = bf16[72,8,1024]{2,1,0:T(8,128)(2,1)S(1)} collective-permute-done((bf16[72,8,1024]{2,1,0:T(8,128)(2,1)}, bf16[72,8,1024]{2,1,0:T(8,128)(2,1)S(1)}, u32[]{:S(2)}, u32[]{:S(2)}) %collective-permute-start.10) | collective-permute-done | bytes 1179680 | tf_op jit(solution)/shard_map/ppermute | solution.py:459
  93.6 1.0 copy-done.2
  94.7 5.4 %shard_map.114 = (bf16[64,32,512]{2,1,0:T(8,128)(2,1)}, bf16[64,32,512]{2,1,0:T(8,128)(2,1)}, bf16[8,32,1024]{2,1,0:T(8,128)(2,1)}) custom-call(s32[2]{0:T(128)} %shifts.9, bf16[64,32,512]{2,1,0:T(8,128)(2,1)} %get-tuple-element.58.updated, bf16[64,32,512]{2,1,0:T(8,128)(2,1)} %get-tuple-element.59.tokens_grad, ...), custom_call_target="tpu_custom_call", output_to_operand_aliasing={{0}: (1, {}), {1}: (2, {})} | custom-call | tf_op jit(solution)/shard_map/pallas_call | solution.py:532
  100.4 0.6 collective-permute-start.13
  101.0 1.4 %collective-permute-start.12 = (bf16[4,2048]{1,0:T(4,128)(2,1)S(1)}, bf16[4,2048]{1,0:T(4,128)(2,1)S(1)}, u32[]{:S(2)}, u32[]{:S(2)}) collective-permute-start(bf16[4,2048]{1,0:T(4,128)(2,1)S(1)} %get-tuple-element.82), channel_id=1, source_target_pairs={{0,1},{1,64},{64,65},{65,0},{2,3},{3,66},{66,67},{67,2},{4,5},{5,6... | collective-permute-start | bytes 49160 | tf_op jit(solution)/shard_map/ppermute | solution.py:468
  102.4 4.3 %collective-permute-done.14 = bf16[4,2048]{1,0:T(4,128)(2,1)S(1)} collective-permute-done((bf16[4,2048]{1,0:T(4,128)(2,1)S(1)}, bf16[4,2048]{1,0:T(4,128)(2,1)S(1)}, u32[]{:S(2)}, u32[]{:S(2)}) %collective-permute-start.14) | collective-permute-done | bytes 16416 | tf_op jit(solution)/shard_map/ppermute | solution.py:468
  106.8 0.6 slice.32
  107.4 0.6 slice.33
  108.0 4.7 %collective-permute-done.11.in_lon = bf16[8,32,1024]{2,1,0:T(8,128)(2,1)S(1)} collective-permute-done((bf16[8,32,1024]{2,1,0:T(8,128)(2,1)}, bf16[8,32,1024]{2,1,0:T(8,128)(2,1)S(1)}, u32[]{:S(2)}, u32[]{:S(2)}) %collective-permute-start.11) | collective-permute-done | bytes 524320 | tf_op jit(solution)/shard_map/ppermute | solution.py:459
  112.7 0.8 copy-done.4
  113.5 3.0 %shard_map.115 = (bf16[64,32,512]{2,1,0:T(8,128)(2,1)}, bf16[64,32,512]{2,1,0:T(8,128)(2,1)}) custom-call(s32[2]{0:T(128)} %shifts.9, bf16[64,32,512]{2,1,0:T(8,128)(2,1)} %get-tuple-element.65.updated, bf16[64,32,512]{2,1,0:T(8,128)(2,1)} %get-tuple-element.66.tokens_grad, bf16[8,32,1024]{2,1,0:T(8,128)(2,1)} %copy-done.4), custom_call_target="tpu_custom_call", output_to_operand_aliasing={{0}: (1, {}), {1}: (2, {})} | custom-call | tf_op jit(solution)/shard_map/pallas_call | solution.py:543
  (40 shorter events, 1.0 us)
Async XLA Ops:
  0.6 1.0 slice-start.2
  0.6 1.2 %slice-start = ((bf16[64,32,512]{2,1,0:T(8,128)(2,1)}), bf16[64,8,512]{2,1,0:T(8,128)(2,1)S(1)}, s32[]{:S(2)}) async-start(bf16[64,32,512]{2,1,0:T(8,128)(2,1)} %tokens_in.3), calls=%async_computation | async-start | bytes 1048576 | tf_op jit(solution)/shard_map/slice | solution.py:554
  0.7 5.9 %slice-start.1 = ((bf16[64,32,512]{2,1,0:T(8,128)(2,1)}), bf16[8,32,512]{2,1,0:T(8,128)(2,1)S(1)}, s32[]{:S(2)}) async-start(bf16[64,32,512]{2,1,0:T(8,128)(2,1)} %tokens_in.3), calls=%async_computation.1 | async-start | bytes 524288 | tf_op jit(solution)/shard_map/slice | solution.py:554
  0.7 5.8 %slice-start.3 = ((bf16[64,32,512]{2,1,0:T(8,128)(2,1)}), bf16[8,32,512]{2,1,0:T(8,128)(2,1)S(1)}, s32[]{:S(2)}) async-start(bf16[64,32,512]{2,1,0:T(8,128)(2,1)} %grads_in.3), calls=%async_computation.3 | async-start | bytes 524288 | tf_op jit(solution)/shard_map/slice | solution.py:554
  0.7 10.9 %copy-start.1 = (bf16[64,32,512]{2,1,0:T(8,128)(2,1)S(1)}, bf16[64,32,512]{2,1,0:T(8,128)(2,1)}, u32[]{:S(2)}) copy-start(bf16[64,32,512]{2,1,0:T(8,128)(2,1)} %grads_in.3) | copy-start | bytes 6291460
  1.8 9.8 %copy-start = (bf16[64,32,512]{2,1,0:T(8,128)(2,1)S(1)}, bf16[64,32,512]{2,1,0:T(8,128)(2,1)}, u32[]{:S(2)}) copy-start(bf16[64,32,512]{2,1,0:T(8,128)(2,1)} %tokens_in.3) | copy-start | bytes 6291460
  2.0 39.4 %collective-permute-start.1 = (bf16[64,8,1024]{2,1,0:T(8,128)(2,1)S(1)}, bf16[64,8,1024]{2,1,0:T(8,128)(2,1)S(1)}, u32[]{:S(2)}, u32[]{:S(2)}) collective-permute-start(bf16[64,8,1024]{2,1,0:T(8,128)(2,1)S(1)} %pad_maximum_fusion), channel_id=1, source_target_pairs={{0,7},{1,0},{2,1},{3,2},{4,3},{5,4},{6,5},{7,6},{8,15},{9,8},{10,9... | collective-permute-start | bytes 3145736 | tf_op jit(solution)/shard_map/ppermute | solution.py:459
  6.6 34.8 %collective-permute-start = (bf16[8,32,1024]{2,1,0:T(8,128)(2,1)S(1)}, bf16[8,32,1024]{2,1,0:T(8,128)(2,1)S(1)}, u32[]{:S(2)}, u32[]{:S(2)}) collective-permute-start(bf16[8,32,1024]{2,1,0:T(8,128)(2,1)S(1)} %pad_maximum_fusion.1), channel_id=1, source_target_pairs={{0,120},{1,121},{2,122},{3,123},{4,124},{5,125},{6,126},{7,127},{8... | collective-permute-start | bytes 1572872 | tf_op jit(solution)/shard_map/ppermute | solution.py:459
  11.6 29.7 %collective-permute-start.2 = (bf16[8,8,1024]{2,1,0:T(8,128)(2,1)S(1)}, bf16[8,8,1024]{2,1,0:T(8,128)(2,1)S(1)}, u32[]{:S(2)}, u32[]{:S(2)}) collective-permute-start(bf16[8,8,1024]{2,1,0:T(8,128)(2,1)S(1)} %pad_maximum_fusion.2), channel_id=1, source_target_pairs={{0,127},{1,120},{2,121},{3,122},{4,123},{5,124},{6,125},{7,126},{8... | collective-permute-start | bytes 393224 | tf_op jit(solution)/shard_map/ppermute | solution.py:459
  41.3 0.7 copy-start.6
  41.3 0.8 copy-start.5
  41.4 1.2 copy-start.3
  60.9 3.0 %collective-permute-start.3 = (bf16[256,2048]{1,0:T(8,128)(2,1)}, bf16[256,2048]{1,0:T(8,128)(2,1)S(1)}, u32[]{:S(2)}, u32[]{:S(2)}) collective-permute-start(bf16[256,2048]{1,0:T(8,128)(2,1)} %get-tuple-element.43), channel_id=1, source_target_pairs={{0,8},{8,0},{1,9},{9,1},{2,10},{10,2},{3,11},{11,3},{4,12},{12,4},... | collective-permute-start | bytes 3145736 | tf_op jit(solution)/shard_map/ppermute | solution.py:571
  61.0 32.6 %collective-permute-start.10 = (bf16[72,8,1024]{2,1,0:T(8,128)(2,1)}, bf16[72,8,1024]{2,1,0:T(8,128)(2,1)S(1)}, u32[]{:S(2)}, u32[]{:S(2)}) collective-permute-start(bf16[72,8,1024]{2,1,0:T(8,128)(2,1)} %get-tuple-element.60), channel_id=1, source_target_pairs={{0,1},{1,2},{2,3},{3,4},{4,5},{5,6},{6,7},{7,0},{8,9},{9,10},{10,1... | collective-permute-start | bytes 3538952 | tf_op jit(solution)/shard_map/ppermute | solution.py:459
  65.6 15.2 %collective-permute-start.4 = (bf16[2,32,2048]{2,1,0:T(8,128)(2,1)S(1)}, bf16[2,32,2048]{2,1,0:T(8,128)(2,1)S(1)}, u32[]{:S(2)}, u32[]{:S(2)}) collective-permute-start(bf16[2,32,2048]{2,1,0:T(8,128)(2,1)S(1)} %get-tuple-element.76), channel_id=1, source_target_pairs={{0,16},{16,32},{32,48},{48,0},{1,17},{17,33},{33,49},{49,1},{2,18}... | collective-permute-start | bytes 786440 | tf_op jit(solution)/shard_map/ppermute | solution.py:468
  65.7 15.2 %collective-permute-start.5 = (bf16[2,32,2048]{2,1,0:T(8,128)(2,1)S(1)}, bf16[2,32,2048]{2,1,0:T(8,128)(2,1)S(1)}, u32[]{:S(2)}, u32[]{:S(2)}) collective-permute-start(bf16[2,32,2048]{2,1,0:T(8,128)(2,1)S(1)} %get-tuple-element.75), channel_id=1, source_target_pairs={{0,32},{16,48},{32,0},{48,16},{1,33},{17,49},{33,1},{49,17},{2,34}... | collective-permute-start | bytes 786440 | tf_op jit(solution)/shard_map/ppermute | solution.py:468
  65.9 15.6 %collective-permute-start.6 = (bf16[2,32,2048]{2,1,0:T(8,128)(2,1)S(1)}, bf16[2,32,2048]{2,1,0:T(8,128)(2,1)S(1)}, u32[]{:S(2)}, u32[]{:S(2)}) collective-permute-start(bf16[2,32,2048]{2,1,0:T(8,128)(2,1)S(1)} %get-tuple-element.74), channel_id=1, source_target_pairs={{0,48},{16,0},{32,16},{48,32},{1,49},{17,1},{33,17},{49,33},{2,50}... | collective-permute-start | bytes 786440 | tf_op jit(solution)/shard_map/ppermute | solution.py:468
  81.6 18.4 %collective-permute-start.7 = (bf16[2,8,2048]{2,1,0:T(8,128)(2,1)S(1)}, bf16[2,8,2048]{2,1,0:T(8,128)(2,1)S(1)}, u32[]{:S(2)}, u32[]{:S(2)}) collective-permute-start(bf16[2,8,2048]{2,1,0:T(8,128)(2,1)S(1)} %get-tuple-element.80), channel_id=1, source_target_pairs={{0,2},{2,4},{4,6},{6,0},{1,3},{3,5},{5,7},{7,1},{8,10},{10,12},{12... | collective-permute-start | bytes 196616 | tf_op jit(solution)/shard_map/ppermute | solution.py:468
  81.7 18.4 %collective-permute-start.8 = (bf16[2,8,2048]{2,1,0:T(8,128)(2,1)S(1)}, bf16[2,8,2048]{2,1,0:T(8,128)(2,1)S(1)}, u32[]{:S(2)}, u32[]{:S(2)}) collective-permute-start(bf16[2,8,2048]{2,1,0:T(8,128)(2,1)S(1)} %get-tuple-element.79), channel_id=1, source_target_pairs={{0,4},{2,6},{4,0},{6,2},{1,5},{3,7},{5,1},{7,3},{8,12},{10,14},{12... | collective-permute-start | bytes 196616 | tf_op jit(solution)/shard_map/ppermute | solution.py:468
  83.9 16.2 %collective-permute-start.9 = (bf16[2,8,2048]{2,1,0:T(8,128)(2,1)S(1)}, bf16[2,8,2048]{2,1,0:T(8,128)(2,1)S(1)}, u32[]{:S(2)}, u32[]{:S(2)}) collective-permute-start(bf16[2,8,2048]{2,1,0:T(8,128)(2,1)S(1)} %get-tuple-element.78), channel_id=1, source_target_pairs={{0,6},{2,0},{4,2},{6,4},{1,7},{3,1},{5,3},{7,5},{8,14},{10,8},{12,... | collective-permute-start | bytes 196616 | tf_op jit(solution)/shard_map/ppermute | solution.py:468
  93.6 1.0 copy-start.2
  100.1 12.6 %collective-permute-start.11 = (bf16[8,32,1024]{2,1,0:T(8,128)(2,1)}, bf16[8,32,1024]{2,1,0:T(8,128)(2,1)S(1)}, u32[]{:S(2)}, u32[]{:S(2)}) collective-permute-start(bf16[8,32,1024]{2,1,0:T(8,128)(2,1)} %get-tuple-element.67), channel_id=1, source_target_pairs={{0,8},{1,9},{2,10},{3,11},{4,12},{5,13},{6,14},{7,15},{8,16},{9,17... | collective-permute-start | bytes 1572872 | tf_op jit(solution)/shard_map/ppermute | solution.py:459
  100.3 6.4 %collective-permute-start.14 = (bf16[4,2048]{1,0:T(4,128)(2,1)S(1)}, bf16[4,2048]{1,0:T(4,128)(2,1)S(1)}, u32[]{:S(2)}, u32[]{:S(2)}) collective-permute-start(bf16[4,2048]{1,0:T(4,128)(2,1)S(1)} %get-tuple-element.83), channel_id=1, source_target_pairs={{0,65},{1,0},{64,1},{65,64},{2,67},{3,2},{66,3},{67,66},{4,69},{5,... | collective-permute-start | bytes 49160 | tf_op jit(solution)/shard_map/ppermute | solution.py:468
  100.4 6.3 %collective-permute-start.13 = (bf16[4,2048]{1,0:T(4,128)(2,1)S(1)}, bf16[4,2048]{1,0:T(4,128)(2,1)S(1)}, u32[]{:S(2)}, u32[]{:S(2)}) collective-permute-start(bf16[4,2048]{1,0:T(4,128)(2,1)S(1)} %get-tuple-element.84), channel_id=1, source_target_pairs={{0,64},{1,65},{64,0},{65,1},{2,66},{3,67},{66,2},{67,3},{4,68},{5,... | collective-permute-start | bytes 49160 | tf_op jit(solution)/shard_map/ppermute | solution.py:468
  101.0 5.8 %collective-permute-start.12 = (bf16[4,2048]{1,0:T(4,128)(2,1)S(1)}, bf16[4,2048]{1,0:T(4,128)(2,1)S(1)}, u32[]{:S(2)}, u32[]{:S(2)}) collective-permute-start(bf16[4,2048]{1,0:T(4,128)(2,1)S(1)} %get-tuple-element.82), channel_id=1, source_target_pairs={{0,1},{1,64},{64,65},{65,0},{2,3},{3,66},{66,67},{67,2},{4,5},{5,6... | collective-permute-start | bytes 49160 | tf_op jit(solution)/shard_map/ppermute | solution.py:468
  112.7 0.8 copy-start.4
where the time goes:
time: 117 us
  Pallas kernels  61.2 us (52%)
  waiting for transfers between devices  26.2 us (22%)
  starting transfers between devices  20.6 us (18%)
  local copies, waits for them, and re-layouts  5.59 us (5%)
  other arithmetic  2 us (2%)
    pallas_call x1, Pallas kernels, run_interior(): call(interior_kernel, [GRID, GRID, sds((D, 4 * D), F32), sds((32, 128), F...  29.4 us
    pallas_call x1, Pallas kernels, run_edge(): call(edge_kernel, [sds(shape, BF) for shape in (lat, lon, lat, lon, (72,...  18.4 us
    ppermute x5, waiting for transfers between devices, shift_to(): return lax.ppermute(value, ALL, pairs)  13.4 us
    ppermute x9, waiting for transfers between devices, scatter_sum(): parts.append(lax.ppermute(block, axes, pairs))  11.9 us
    ppermute x5, starting transfers between devices, shift_to(): return lax.ppermute(value, ALL, pairs)  11.8 us
    ppermute x9, starting transfers between devices, scatter_sum(): parts.append(lax.ppermute(block, axes, pairs))  8.72 us
    pallas_call x1, Pallas kernels, run_lat_return(): call(lat_return_kernel, [GRID, GRID, sds((8, 32, 2 * D), BF)], [vmem((2,...  5.37 us
    pallas_call x1, Pallas kernels, run_edge_merge(): call(edge_merge_kernel, [GRID, GRID], [vmem((2, 64, 16, D), BF), vmem((2,...  5.06 us
  transfers between devices with their start and end apart: 15, of which 7 were waited for; matrix products, arithmetic and copies ran while one was open for 3% of the time, Pallas kernels for 34%

commit v1 on v0

--- a/solution.py
+++ b/solution.py
@@ -46,15 +46,11 @@
     xg[at, :] = g.astype(BF)
 
 
-def project_rows(first, count, hid, xg, w_qkv, w_out, qkvg):
-    at = pl.ds(first, count)
-    qkvg[at, : 3 * D] = dot_nn(hid[at, :], w_qkv[...]).astype(BF)
-    qkvg[at, 3 * D :] = dot_nt(xg[at, :], w_out[...]).astype(BF)
-
-
 def project(rows, chunk, hid, xg, w_qkv, w_out, qkvg):
     def step(c, carry):
-        project_rows(pl.multiple_of(c * chunk, 64), chunk, hid, xg, w_qkv, w_out, qkvg)
+        at = pl.ds(pl.multiple_of(c * chunk, 64), chunk)
+        qkvg[at, : 3 * D] = dot_nn(hid[at, :], w_qkv[...]).astype(BF)
+        qkvg[at, 3 * D :] = dot_nt(xg[at, :], w_out[...]).astype(BF)
         return carry
 
     lax.fori_loop(0, rows // chunk, step, 0)
@@ -247,7 +243,7 @@
 
 def edge_kernel(
     shifts, tokens_in, grads_in, halo_lon, halo_lat, halo_cor, keys, bias, w_qkv_in, w_out_in, w_part,
-    lat_up, lon_up, lat_grad, lon_grad, out_lat, out_lon, w_mine, w_other,
+    lat_up, lon_up, lat_grad, lon_grad, out_up, out_grad, out_lon, out_cor, w_mine, w_other,
     tok, grad, far, low_tok, low_grad, low_far, w_qkv, w_out, to_lat, to_lon,
     xt, xg, hid, istd, qkvg, mix, dq, ones, w_sum, sems,
 ):
@@ -328,7 +324,9 @@
             (grad, lat_grad),
             (low_tok.at[0:8], lon_up),
             (low_grad.at[0:8], lon_grad),
-            (to_lat, out_lat),
+            (to_lat.at[0:64, :, 0:D], out_up),
+            (to_lat.at[0:64, :, D : 2 * D], out_grad),
+            (to_lat.at[64:72], out_cor),
             (to_lon, out_lon),
         ],
         sems,
@@ -376,40 +374,45 @@
     wait_all(start_all([(b, a) for a, b in pairs], sems))
 
 
-def lat_return_kernel(
-    shifts, updated, tokens_grad, in_lat, out_lon, out_updated, out_grad, to_lon, side, sems
+def place_lat(s1, came, side):
+    mark = iota((8, 8, D), 1) < s1
+
+    def place(r, carry):
+        at = pl.ds(pl.multiple_of(r * 8, 8), 8)
+        rows = side[at, 0:8, :].astype(F32)
+        side[at, 0:8, :] = jnp.where(mark, came[at, :, :].astype(F32), rows).astype(BF)
+        return carry
+
+    lax.fori_loop(0, 8, place, 0)
+
+
+def updated_return_kernel(shifts, updated, in_up, out_updated, side, sems):
+    pairs = [(out_updated.at[:, 0:16, :], side)]
+    wait_all(start_all(pairs, sems))
+    place_lat(shifts[1], in_up, side)
+    wait_all(start_all([(b, a) for a, b in pairs], sems))
+
+
+def return_kernel(
+    shifts, updated, tokens_grad, in_grad, in_lon, in_cor, out_updated, out_grad, side, top, sems
 ):
-    s1 = shifts[1]
-    pairs = [(out.at[:, 0:16, :], side.at[n]) for n, out in enumerate((out_updated, out_grad))]
-    copies = start_all(pairs, sems)
-    mark = iota((8, 8, D), 1) < s1
+    s0, s1 = shifts[0], shifts[1]
+    pairs = [(out_grad.at[8:64, 0:16, :], side.at[8:64])]
+    pairs += [(out.at[0:8], top.at[n]) for n, out in enumerate((out_updated, out_grad))]
+    wait_all(start_all(pairs, sems))
+    place_lat(s1, in_grad, side)
+    early = iota((8, 32, D), 0) < s0
+    first = iota((8, 8, D), 1) < s1
     for n in range(2):
         cols = slice(n * D, n * D + D)
-        first = jnp.where(mark, in_lat[64:72, :, cols].astype(F32), out_lon[:, 0:8, cols].astype(F32))
-        to_lon[:, 0:8, cols] = first.astype(BF)
-        to_lon[:, 8:32, cols] = out_lon[:, 8:32, cols]
-    wait_all(copies)
-    for n in range(2):
-
-        def place(r, carry, n=n):
-            at = pl.ds(pl.multiple_of(r * 8, 8), 8)
-            rows = side[n, at, 0:8, :].astype(F32)
-            came = in_lat[at, :, n * D : n * D + D].astype(F32)
-            side[n, at, 0:8, :] = jnp.where(mark, came, rows).astype(BF)
-            return carry
-
-        lax.fori_loop(0, 8, place, 0)
-    wait_all(start_all([(b, a) for a, b in pairs], sems))
-
-
-def lon_return_kernel(shifts, updated, tokens_grad, in_lon, out_updated, out_grad, top, sems):
-    s0 = shifts[0]
-    pairs = [(out.at[0:8], top.at[n]) for n, out in enumerate((out_updated, out_grad))]
-    wait_all(start_all(pairs, sems))
-    early = iota((8, 32, D), 0) < s0
-    for n in range(2):
-        came = in_lon[:, :, n * D : n * D + D].astype(F32)
-        top[n] = jnp.where(early, came, top[n].astype(F32)).astype(BF)
+        came = in_lon[:, :, cols].astype(F32)
+        corner = jnp.where(first, in_cor[:, :, cols].astype(F32), came[:, 0:8])
+        came = jnp.concatenate([corner, came[:, 8:]], axis=1)
+        old = top[n].astype(F32)
+        if n == 1:
+            back = jnp.where(first, in_grad[0:8, :, :].astype(F32), old[:, 0:8])
+            old = jnp.concatenate([back, old[:, 8:]], axis=1)
+        top[n] = jnp.where(early, came, old).astype(BF)
     wait_all(start_all([(b, a) for a, b in pairs], sems))
 
 
@@ -500,10 +503,10 @@
 
 def run_edge(*args):
     lat, lon = (64, 16, D), (8, 32, D)
-    far_lat, far_lon = (64, 8, 2 * D), (8, 32, 2 * D)
+    near, far_lat, far_lon = (64, 8, D), (64, 8, 2 * D), (8, 32, 2 * D)
     return call(
         edge_kernel,
-        [sds(shape, BF) for shape in (lat, lon, lat, lon, (72, 8, 2 * D), far_lon)]
+        [sds(shape, BF) for shape in (lat, lon, lat, lon, near, near, far_lon, (8, 8, 2 * D))]
         + [sds((D // 2, 4 * D), BF)] * 2,
         [vmem(lat, BF), vmem(lat, BF), vmem(far_lat, BF)]
         + [vmem((16, 32, D), BF), vmem((16, 32, D), BF), vmem((16, 8, 2 * D), BF)]
@@ -513,7 +516,7 @@
         + attend_scratch(OUTER)
         + [vmem((D, 4 * D), F32), DMA((12,))],
         [IN_HBM] * 5 + [IN_VMEM] * 2 + [IN_HBM] * 3,
-        [IN_HBM] * 6 + [IN_VMEM] * 2,
+        [IN_HBM] * 8 + [IN_VMEM] * 2,
     )(*args)
 
 
@@ -528,23 +531,17 @@
     )(*args)
 
 
-def run_lat_return(*args):
+def run_updated_return(*args):
+    scratch = [vmem((64, 16, D), BF), DMA((1,))]
+    return call(updated_return_kernel, GRID, scratch, [IN_HBM, IN_VMEM], IN_HBM, {1: 0})(*args)
+
+
+def run_return(*args):
     return call(
-        lat_return_kernel,
-        [GRID, GRID, sds((8, 32, 2 * D), BF)],
-        [vmem((2, 64, 16, D), BF), DMA((2,))],
-        [IN_HBM] * 2 + [IN_VMEM] * 2,
-        [IN_HBM] * 2 + [IN_VMEM],
-        {1: 0, 2: 1},
-    )(*args)
-
-
-def run_lon_return(*args):
-    return call(
-        lon_return_kernel,
+        return_kernel,
         [GRID, GRID],
-        [vmem((2, 8, 32, D), BF), DMA((2,))],
-        [IN_HBM] * 2 + [IN_VMEM],
+        [vmem((64, 16, D), BF), vmem((2, 8, 32, D), BF), DMA((3,))],
+        [IN_HBM] * 2 + [IN_VMEM] * 3,
         [IN_HBM] * 2,
         {1: 0, 2: 1},
     )(*args)
@@ -559,26 +556,28 @@
     updated, tokens_grad, w_part, keys, bias = run_interior(
         shifts, tokens, grad_out, pad_mask, bias_table, rel_index, w_qkv, w_out
     )
-    *edges, out_lat, out_lon, w_mine, w_other = run_edge(
+    *edges, out_up, out_grad, out_lon, out_cor, w_mine, w_other = run_edge(
         shifts, tokens, grad_out, halo_lon, halo_lat, halo_cor, keys, bias, w_qkv, w_out, w_part
     )
 
     def merge_beside(blocks):
         _, *placed = lax.optimization_barrier((blocks, updated, tokens_grad))
-        return run_edge_merge(shifts, *placed, *edges)
-
-    in_lat = shift_to(out_lat, 0, 1)
+        placed, grad = run_edge_merge(shifts, *placed, *edges)
+        return run_updated_return(shifts, placed, in_up), grad
+
     w_got = lax.ppermute(w_other, "core", [(0, 1), (1, 0)])
+    in_up = shift_to(out_up, 0, 1)
+    in_grad = shift_to(out_grad, 0, 1)
+    in_lon = shift_to(out_lon, 1, 0)
+    in_cor = shift_to(out_cor, 1, 1)
     total = (w_mine.astype(F32) + w_got.astype(F32)).astype(BF)
     total = total.reshape(2, 4, 32, 4 * D).transpose(1, 0, 2, 3)
     total, (updated, tokens_grad) = scatter_sum(total, "x", 4, merge_beside)
     total = total.astype(BF).reshape(2, 4, 8, 4 * D).transpose(1, 0, 2, 3)
-    lat_beside = lambda blocks: run_lat_return(shifts, updated, tokens_grad, in_lat, out_lon)
-    total, (updated, tokens_grad, out_lon) = scatter_sum(total, "y", 4, lat_beside)
-    in_lon = shift_to(out_lon, 1, 0)
+    total, (in_grad, in_cor) = scatter_sum(total, "y", 4, lambda blocks: (in_grad, in_cor))
     total, _ = scatter_sum(total.astype(BF).reshape(4, 4, 4 * D), ("zh", "zl"), 4)
 
-    updated, tokens_grad = run_lon_return(shifts, updated, tokens_grad, in_lon)
+    updated, tokens_grad = run_return(shifts, updated, tokens_grad, in_grad, in_lon, in_cor)
     return (updated, tokens_grad, total[:, : 3 * D], total[:, 3 * D :])
 
 

time: 117 us -> 108 us (0.923)
  waiting for transfers between devices: 26.2 us -> 9.43 us
  starting transfers between devices: 20.6 us -> 28.8 us
    ppermute x9, waiting for transfers between devices: 11.9 us -> 0.02 us  [scatter_sum(): parts.append(lax.ppermute(block, axes, pairs))]
    ppermute x5 -> x7, starting transfers between devices: 11.8 us -> 18.8 us  [shift_to(): return lax.ppermute(value, ALL, pairs)]
    ppermute x5 -> x7, waiting for transfers between devices: 13.4 us -> 8.47 us  [shift_to(): return lax.ppermute(value, ALL, pairs)]
    ppermute x9, starting transfers between devices: 8.72 us -> 9.93 us  [scatter_sum(): parts.append(lax.ppermute(block, axes, pairs))]
    unnamed x14 -> x20, local copies, waits for them, and re-layouts: 3 us -> 2.79 us
  transfers between devices with their start and end apart: 15 -> 17, of which waited for: 7 -> 4; matrix products, arithmetic and copies ran while one was open for 3% -> 2% of each run, Pallas kernels for 34% -> 39%
where the time goes in v1:
time: 108 us; the launch traced here: 107 us
  Pallas kernels  60.1 us (56%)
  starting transfers between devices  28.8 us (27%)
  waiting for transfers between devices  9.43 us (9%)
  local copies, waits for them, and re-layouts  5.39 us (5%)
  other arithmetic  2.01 us (2%)
    pallas_call x1, Pallas kernels, run_interior(): call(interior_kernel, [GRID, GRID, sds((D, 4 * D), F32), sds((32, 128), F...  29.4 us
    ppermute x7, starting transfers between devices, shift_to(): return lax.ppermute(value, ALL, pairs)  18.8 us
    pallas_call x1, Pallas kernels, run_edge(): call(edge_kernel, [sds(shape, BF) for shape in (lat, lon, lat, lon, near,...  18.4 us
    ppermute x9, starting transfers between devices, scatter_sum(): parts.append(lax.ppermute(block, axes, pairs))  9.93 us
    ppermute x7, waiting for transfers between devices, shift_to(): return lax.ppermute(value, ALL, pairs)  8.47 us
    pallas_call x1, Pallas kernels, run_edge_merge(): call(edge_merge_kernel, [GRID, GRID], [vmem((2, 64, 16, D), BF), vmem((2,...  5.06 us
    pallas_call x1, Pallas kernels, run_return(): call(return_kernel, [GRID, GRID], [vmem((64, 16, D), BF), vmem((2, 8, 32,...  3.79 us
    pallas_call x1, Pallas kernels, run_updated_return(): call(updated_return_kernel, GRID, scratch, [IN_HBM, IN_VMEM], IN_HBM, {1:...  3.45 us
  transfers between devices with their start and end apart: 17, of which 4 were waited for; matrix products, arithmetic and copies ran while one was open for 2% of the time, Pallas kernels for 39%

profile of v1, /device:TPU:0, one launch (start us, length us, event | category | flops | bytes accessed | tf_op | source)
XLA Modules:
  0.0 106.7 jit_solution(17131967708602970764)
XLA Ops:
  0.7 1.0 slice-done.2
  1.7 0.2 slice-done
  2.0 4.5 %collective-permute-start.1 = (bf16[64,8,1024]{2,1,0:T(8,128)(2,1)S(1)}, bf16[64,8,1024]{2,1,0:T(8,128)(2,1)S(1)}, u32[]{:S(2)}, u32[]{:S(2)}) collective-permute-start(bf16[64,8,1024]{2,1,0:T(8,128)(2,1)S(1)} %pad_maximum_fusion), channel_id=1, source_target_pairs={{0,7},{1,0},{2,1},{3,2},{4,3},{5,4},{6,5},{7,6},{8,15},{9,8},{10,9... | collective-permute-start | bytes 3145736 | tf_op jit(solution)/shard_map/ppermute | solution.py:462
  6.6 5.0 %collective-permute-start = (bf16[8,32,1024]{2,1,0:T(8,128)(2,1)S(1)}, bf16[8,32,1024]{2,1,0:T(8,128)(2,1)S(1)}, u32[]{:S(2)}, u32[]{:S(2)}) collective-permute-start(bf16[8,32,1024]{2,1,0:T(8,128)(2,1)S(1)} %pad_maximum_fusion.1), channel_id=1, source_target_pairs={{0,120},{1,121},{2,122},{3,123},{4,124},{5,125},{6,126},{7,127},{8... | collective-permute-start | bytes 1572872 | tf_op jit(solution)/shard_map/ppermute | solution.py:462
  11.6 0.3 collective-permute-start.2
  11.9 29.4 %shard_map.111 = (bf16[64,32,512]{2,1,0:T(8,128)(2,1)}, bf16[64,32,512]{2,1,0:T(8,128)(2,1)}, f32[512,2048]{1,0:T(8,128)}, f32[32,128]{1,0:T(8,128)}, f32[64,512]{1,0:T(8,128)}) custom-call(s32[2]{0:T(128)} %shifts.9, bf16[64,32,512]{2,1,0:T(8,128)(2,1)} %tokens_in.3, bf16[64,32,512]{2,1,0:T(8,128)(2,1)} %grads_in.3, s32[1024,256]{1,0:T(8,128)} %pad_in.1, ...), custom_call_target="tpu_custom_call" | custom-call | tf_op jit(solution)/shard_map/pallas_call | solution.py:492
  41.4 0.6 copy-done.7
  42.0 0.2 copy-done.4
  42.2 0.4 copy-done.2
  42.5 18.4 %shard_map.112 = (bf16[64,16,512]{2,1,0:T(8,128)(2,1)}, bf16[8,32,512]{2,1,0:T(8,128)(2,1)}, bf16[64,16,512]{2,1,0:T(8,128)(2,1)}, bf16[8,32,512]{2,1,0:T(8,128)...) custom-call(s32[2]{0:T(128)} %shifts.9, ...), custom_call_target="tpu_custom_call" | custom-call | tf_op jit(solution)/shard_map/pallas_call | solution.py:507
  61.1 1.9 %collective-permute-start.7 = (bf16[64,8,512]{2,1,0:T(8,128)(2,1)}, bf16[64,8,512]{2,1,0:T(8,128)(2,1)S(1)}, u32[]{:S(2)}, u32[]{:S(2)}) collective-permute-start(bf16[64,8,512]{2,1,0:T(8,128)(2,1)} %get-tuple-element.51), channel_id=1, source_target_pairs={{0,1},{1,2},{2,3},{3,4},{4,5},{5,6},{6,7},{7,0},{8,9},{9,10},{10,1... | collective-permute-start | bytes 1572872 | tf_op jit(solution)/shard_map/ppermute | solution.py:462
  62.9 0.9 collective-permute-done.3
  63.9 1.6 %add_convert_fusion = bf16[256,2048]{1,0:T(8,128)(2,1)S(1)} fusion(bf16[256,2048]{1,0:T(8,128)(2,1)S(1)} %collective-permute-done.3, bf16[256,2048]{1,0:T(8,128)(2,1)} %get-tuple-element.40), kind=kLoop, calls=%fused_computation | loop fusion | flops 2097152 | bytes 3145728 | tf_op jit(solution)/shard_map/convert_element_type | solution.py:573
  65.7 0.2 collective-permute-start.5
  65.9 3.0 %collective-permute-start.6 = (bf16[2,32,2048]{2,1,0:T(8,128)(2,1)S(1)}, bf16[2,32,2048]{2,1,0:T(8,128)(2,1)S(1)}, u32[]{:S(2)}, u32[]{:S(2)}) collective-permute-start(bf16[2,32,2048]{2,1,0:T(8,128)(2,1)S(1)} %get-tuple-element.70), channel_id=1, source_target_pairs={{0,48},{16,0},{32,16},{48,32},{1,49},{17,1},{33,17},{49,33},{2,50}... | collective-permute-start | bytes 786440 | tf_op jit(solution)/shard_map/ppermute | solution.py:471
  68.9 1.6 %collective-permute-start.11 = (bf16[64,8,512]{2,1,0:T(8,128)(2,1)}, bf16[64,8,512]{2,1,0:T(8,128)(2,1)S(1)}, u32[]{:S(2)}, u32[]{:S(2)}) collective-permute-start(bf16[64,8,512]{2,1,0:T(8,128)(2,1)} %get-tuple-element.59), channel_id=1, source_target_pairs={{0,1},{1,2},{2,3},{3,4},{4,5},{5,6},{6,7},{7,0},{8,9},{9,10},{10,1... | collective-permute-start | bytes 1572872 | tf_op jit(solution)/shard_map/ppermute | solution.py:462
  70.5 5.1 %shard_map.113 = (bf16[64,32,512]{2,1,0:T(8,128)(2,1)}, bf16[64,32,512]{2,1,0:T(8,128)(2,1)}) custom-call(s32[2]{0:T(128)} %shifts.9, bf16[64,32,512]{2,1,0:T(8,128)(2,1)} %get-tuple-element.44.updated, bf16[64,32,512]{2,1,0:T(8,128)(2,1)} %get-tuple-element.45.tokens_grad, ...), custom_call_target="tpu_custom_call", output_to_operand_aliasing={{0}: (1, {}), {1}: (2, {})} | custom-call | tf_op jit(solution)/shard_map/pallas_call | solution.py:524
  75.6 2.7 %collective-permute-done.7.in_up = bf16[64,8,512]{2,1,0:T(8,128)(2,1)S(1)} collective-permute-done((bf16[64,8,512]{2,1,0:T(8,128)(2,1)}, bf16[64,8,512]{2,1,0:T(8,128)(2,1)S(1)}, u32[]{:S(2)}, u32[]{:S(2)}) %collective-permute-start.7) | collective-permute-done | bytes 524320 | tf_op jit(solution)/shard_map/ppermute | solution.py:462
  78.2 0.8 copy-done.3
  79.0 3.5 %shard_map.114.updated = bf16[64,32,512]{2,1,0:T(8,128)(2,1)} custom-call(s32[2]{0:T(128)} %shifts.9, bf16[64,32,512]{2,1,0:T(8,128)(2,1)} %get-tuple-element.50.updated, bf16[64,8,512]{2,1,0:T(8,128)(2,1)} %copy-done.3), custom_call_target="tpu_custom_call", output_to_operand_aliasing={{}: (1, {})} | custom-call | tf_op jit(solution)/shard_map/pallas_call | solution.py:536
  82.5 0.1 fusion
  82.8 1.2 %collective-permute-start.9 = (bf16[2,8,2048]{2,1,0:T(8,128)(2,1)S(1)}, bf16[2,8,2048]{2,1,0:T(8,128)(2,1)S(1)}, u32[]{:S(2)}, u32[]{:S(2)}) collective-permute-start(bf16[2,8,2048]{2,1,0:T(8,128)(2,1)S(1)} %get-tuple-element.75), channel_id=1, source_target_pairs={{0,4},{2,6},{4,0},{6,2},{1,5},{3,7},{5,1},{7,3},{8,12},{10,14},{12... | collective-permute-start | bytes 196616 | tf_op jit(solution)/shard_map/ppermute | solution.py:471
  83.9 2.0 %collective-permute-start.10 = (bf16[2,8,2048]{2,1,0:T(8,128)(2,1)S(1)}, bf16[2,8,2048]{2,1,0:T(8,128)(2,1)S(1)}, u32[]{:S(2)}, u32[]{:S(2)}) collective-permute-start(bf16[2,8,2048]{2,1,0:T(8,128)(2,1)S(1)} %get-tuple-element.74), channel_id=1, source_target_pairs={{0,6},{2,0},{4,2},{6,4},{1,7},{3,1},{5,3},{7,5},{8,14},{10,8},{12,... | collective-permute-start | bytes 196616 | tf_op jit(solution)/shard_map/ppermute | solution.py:471
  86.0 2.4 %collective-permute-done.12.in_cor = bf16[8,8,1024]{2,1,0:T(8,128)(2,1)S(1)} collective-permute-done((bf16[8,8,1024]{2,1,0:T(8,128)(2,1)}, bf16[8,8,1024]{2,1,0:T(8,128)(2,1)S(1)}, u32[]{:S(2)}, u32[]{:S(2)}) %collective-permute-start.12) | collective-permute-done | bytes 131104 | tf_op jit(solution)/shard_map/ppermute | solution.py:462
  88.4 5.5 %collective-permute-start.13 = (bf16[8,32,1024]{2,1,0:T(8,128)(2,1)S(1)}, bf16[8,32,1024]{2,1,0:T(8,128)(2,1)S(1)}, u32[]{:S(2)}, u32[]{:S(2)}) collective-permute-start(bf16[8,32,1024]{2,1,0:T(8,128)(2,1)S(1)} %copy-done.9), channel_id=1, source_target_pairs={{0,8},{1,9},{2,10},{3,11},{4,12},{5,13},{6,14},{7,15},{8,16},{9,17... | collective-permute-start | bytes 1572872 | tf_op jit(solution)/shard_map/ppermute | solution.py:462
  94.0 0.2 collective-permute-start.16
  94.2 3.1 %collective-permute-start.15 = (bf16[4,2048]{1,0:T(4,128)(2,1)S(1)}, bf16[4,2048]{1,0:T(4,128)(2,1)S(1)}, u32[]{:S(2)}, u32[]{:S(2)}) collective-permute-start(bf16[4,2048]{1,0:T(4,128)(2,1)S(1)} %get-tuple-element.80), channel_id=1, source_target_pairs={{0,64},{1,65},{64,0},{65,1},{2,66},{3,67},{66,2},{67,3},{4,68},{5,... | collective-permute-start | bytes 49160 | tf_op jit(solution)/shard_map/ppermute | solution.py:471
  97.3 3.4 %collective-permute-done.13.in_lon = bf16[8,32,1024]{2,1,0:T(8,128)(2,1)S(1)} collective-permute-done((bf16[8,32,1024]{2,1,0:T(8,128)(2,1)S(1)}, bf16[8,32,1024]{2,1,0:T(8,128)(2,1)S(1)}, u32[]{:S(2)}, u32[]{:S(2)}) %collective-permute-start.13) | collective-permute-done | bytes 524320 | tf_op jit(solution)/shard_map/ppermute | solution.py:462
  100.8 0.8 copy-done.6
  101.6 3.8 %shard_map.115 = (bf16[64,32,512]{2,1,0:T(8,128)(2,1)}, bf16[64,32,512]{2,1,0:T(8,128)(2,1)}) custom-call(s32[2]{0:T(128)} %shifts.9, bf16[64,32,512]{2,1,0:T(8,128)(2,1)} %shard_map.114.updated, bf16[64,32,512]{2,1,0:T(8,128)(2,1)} %get-tuple-element.54.tokens_grad, bf16[64,8,512]{2,1,0:T(8,128)(2,1)} %copy-done.5, ...), custom_call_target="tpu_custom_call", output_to_operand_aliasing={{0}: (1, {}), {1}: (2, {})} | custom-call | tf_op jit(solution)/shard_map/pallas_call | solution.py:540
  105.5 0.6 slice.32
  106.1 0.6 slice.33
  (50 shorter events, 0.8 us)
Async XLA Ops:
  0.6 1.0 slice-start.2
  0.6 1.2 %slice-start = ((bf16[64,32,512]{2,1,0:T(8,128)(2,1)}), bf16[64,8,512]{2,1,0:T(8,128)(2,1)S(1)}, s32[]{:S(2)}) async-start(bf16[64,32,512]{2,1,0:T(8,128)(2,1)} %tokens_in.3), calls=%async_computation | async-start | bytes 1048576 | tf_op jit(solution)/shard_map/slice | solution.py:551
  0.7 5.9 %slice-start.1 = ((bf16[64,32,512]{2,1,0:T(8,128)(2,1)}), bf16[8,32,512]{2,1,0:T(8,128)(2,1)S(1)}, s32[]{:S(2)}) async-start(bf16[64,32,512]{2,1,0:T(8,128)(2,1)} %tokens_in.3), calls=%async_computation.1 | async-start | bytes 524288 | tf_op jit(solution)/shard_map/slice | solution.py:551
  0.7 5.8 %slice-start.3 = ((bf16[64,32,512]{2,1,0:T(8,128)(2,1)}), bf16[8,32,512]{2,1,0:T(8,128)(2,1)S(1)}, s32[]{:S(2)}) async-start(bf16[64,32,512]{2,1,0:T(8,128)(2,1)} %grads_in.3), calls=%async_computation.3 | async-start | bytes 524288 | tf_op jit(solution)/shard_map/slice | solution.py:551
  0.7 10.9 %copy-start.1 = (bf16[64,32,512]{2,1,0:T(8,128)(2,1)S(1)}, bf16[64,32,512]{2,1,0:T(8,128)(2,1)}, u32[]{:S(2)}) copy-start(bf16[64,32,512]{2,1,0:T(8,128)(2,1)} %grads_in.3) | copy-start | bytes 6291460
  1.8 9.8 %copy-start = (bf16[64,32,512]{2,1,0:T(8,128)(2,1)S(1)}, bf16[64,32,512]{2,1,0:T(8,128)(2,1)}, u32[]{:S(2)}) copy-start(bf16[64,32,512]{2,1,0:T(8,128)(2,1)} %tokens_in.3) | copy-start | bytes 6291460
  2.0 39.4 %collective-permute-start.1 = (bf16[64,8,1024]{2,1,0:T(8,128)(2,1)S(1)}, bf16[64,8,1024]{2,1,0:T(8,128)(2,1)S(1)}, u32[]{:S(2)}, u32[]{:S(2)}) collective-permute-start(bf16[64,8,1024]{2,1,0:T(8,128)(2,1)S(1)} %pad_maximum_fusion), channel_id=1, source_target_pairs={{0,7},{1,0},{2,1},{3,2},{4,3},{5,4},{6,5},{7,6},{8,15},{9,8},{10,9... | collective-permute-start | bytes 3145736 | tf_op jit(solution)/shard_map/ppermute | solution.py:462
  6.6 34.8 %collective-permute-start = (bf16[8,32,1024]{2,1,0:T(8,128)(2,1)S(1)}, bf16[8,32,1024]{2,1,0:T(8,128)(2,1)S(1)}, u32[]{:S(2)}, u32[]{:S(2)}) collective-permute-start(bf16[8,32,1024]{2,1,0:T(8,128)(2,1)S(1)} %pad_maximum_fusion.1), channel_id=1, source_target_pairs={{0,120},{1,121},{2,122},{3,123},{4,124},{5,125},{6,126},{7,127},{8... | collective-permute-start | bytes 1572872 | tf_op jit(solution)/shard_map/ppermute | solution.py:462
  11.6 29.7 %collective-permute-start.2 = (bf16[8,8,1024]{2,1,0:T(8,128)(2,1)S(1)}, bf16[8,8,1024]{2,1,0:T(8,128)(2,1)S(1)}, u32[]{:S(2)}, u32[]{:S(2)}) collective-permute-start(bf16[8,8,1024]{2,1,0:T(8,128)(2,1)S(1)} %pad_maximum_fusion.2), channel_id=1, source_target_pairs={{0,127},{1,120},{2,121},{3,122},{4,123},{5,124},{6,125},{7,126},{8... | collective-permute-start | bytes 393224 | tf_op jit(solution)/shard_map/ppermute | solution.py:462
  41.3 0.7 copy-start.7
  41.3 0.8 copy-start.4
  41.4 1.2 %copy-start.2 = (bf16[64,8,1024]{2,1,0:T(8,128)(2,1)}, bf16[64,8,1024]{2,1,0:T(8,128)(2,1)S(1)}, u32[]{:S(2)}) copy-start(bf16[64,8,1024]{2,1,0:T(8,128)(2,1)S(1)} %collective-permute-done.1.halo_lat) | copy-start | bytes 3145732
  60.9 3.0 %collective-permute-start.3 = (bf16[256,2048]{1,0:T(8,128)(2,1)}, bf16[256,2048]{1,0:T(8,128)(2,1)S(1)}, u32[]{:S(2)}, u32[]{:S(2)}) collective-permute-start(bf16[256,2048]{1,0:T(8,128)(2,1)} %get-tuple-element.41), channel_id=1, source_target_pairs={{0,8},{8,0},{1,9},{9,1},{2,10},{10,2},{3,11},{11,3},{4,12},{12,4},... | collective-permute-start | bytes 3145736 | tf_op jit(solution)/shard_map/ppermute | solution.py:568
  61.1 17.1 %collective-permute-start.7 = (bf16[64,8,512]{2,1,0:T(8,128)(2,1)}, bf16[64,8,512]{2,1,0:T(8,128)(2,1)S(1)}, u32[]{:S(2)}, u32[]{:S(2)}) collective-permute-start(bf16[64,8,512]{2,1,0:T(8,128)(2,1)} %get-tuple-element.51), channel_id=1, source_target_pairs={{0,1},{1,2},{2,3},{3,4},{4,5},{5,6},{6,7},{7,0},{8,9},{9,10},{10,1... | collective-permute-start | bytes 1572872 | tf_op jit(solution)/shard_map/ppermute | solution.py:462
  65.6 16.9 %collective-permute-start.4 = (bf16[2,32,2048]{2,1,0:T(8,128)(2,1)S(1)}, bf16[2,32,2048]{2,1,0:T(8,128)(2,1)S(1)}, u32[]{:S(2)}, u32[]{:S(2)}) collective-permute-start(bf16[2,32,2048]{2,1,0:T(8,128)(2,1)S(1)} %get-tuple-element.72), channel_id=1, source_target_pairs={{0,16},{16,32},{32,48},{48,0},{1,17},{17,33},{33,49},{49,1},{2,18}... | collective-permute-start | bytes 786440 | tf_op jit(solution)/shard_map/ppermute | solution.py:471
  65.7 16.8 %collective-permute-start.5 = (bf16[2,32,2048]{2,1,0:T(8,128)(2,1)S(1)}, bf16[2,32,2048]{2,1,0:T(8,128)(2,1)S(1)}, u32[]{:S(2)}, u32[]{:S(2)}) collective-permute-start(bf16[2,32,2048]{2,1,0:T(8,128)(2,1)S(1)} %get-tuple-element.71), channel_id=1, source_target_pairs={{0,32},{16,48},{32,0},{48,16},{1,33},{17,49},{33,1},{49,17},{2,34}... | collective-permute-start | bytes 786440 | tf_op jit(solution)/shard_map/ppermute | solution.py:471
  65.9 16.6 %collective-permute-start.6 = (bf16[2,32,2048]{2,1,0:T(8,128)(2,1)S(1)}, bf16[2,32,2048]{2,1,0:T(8,128)(2,1)S(1)}, u32[]{:S(2)}, u32[]{:S(2)}) collective-permute-start(bf16[2,32,2048]{2,1,0:T(8,128)(2,1)S(1)} %get-tuple-element.70), channel_id=1, source_target_pairs={{0,48},{16,0},{32,16},{48,32},{1,49},{17,1},{33,17},{49,33},{2,50}... | collective-permute-start | bytes 786440 | tf_op jit(solution)/shard_map/ppermute | solution.py:471
  68.9 24.9 %collective-permute-start.11 = (bf16[64,8,512]{2,1,0:T(8,128)(2,1)}, bf16[64,8,512]{2,1,0:T(8,128)(2,1)S(1)}, u32[]{:S(2)}, u32[]{:S(2)}) collective-permute-start(bf16[64,8,512]{2,1,0:T(8,128)(2,1)} %get-tuple-element.59), channel_id=1, source_target_pairs={{0,1},{1,2},{2,3},{3,4},{4,5},{5,6},{6,7},{7,0},{8,9},{9,10},{10,1... | collective-permute-start | bytes 1572872 | tf_op jit(solution)/shard_map/ppermute | solution.py:462
  78.2 0.8 copy-start.3
  78.2 10.1 %collective-permute-start.12 = (bf16[8,8,1024]{2,1,0:T(8,128)(2,1)}, bf16[8,8,1024]{2,1,0:T(8,128)(2,1)S(1)}, u32[]{:S(2)}, u32[]{:S(2)}) collective-permute-start(bf16[8,8,1024]{2,1,0:T(8,128)(2,1)} %get-tuple-element.60), channel_id=1, source_target_pairs={{0,9},{1,10},{2,11},{3,12},{4,13},{5,14},{6,15},{7,8},{8,17},{9,18... | collective-permute-start | bytes 393224 | tf_op jit(solution)/shard_map/ppermute | solution.py:462
  79.0 9.4 %copy-start.9 = (bf16[8,32,1024]{2,1,0:T(8,128)(2,1)S(1)}, bf16[8,32,1024]{2,1,0:T(8,128)(2,1)}, u32[]{:S(2)}) copy-start(bf16[8,32,1024]{2,1,0:T(8,128)(2,1)} %get-tuple-element.62) | copy-start | bytes 1572868
  82.7 11.2 %collective-permute-start.8 = (bf16[2,8,2048]{2,1,0:T(8,128)(2,1)S(1)}, bf16[2,8,2048]{2,1,0:T(8,128)(2,1)S(1)}, u32[]{:S(2)}, u32[]{:S(2)}) collective-permute-start(bf16[2,8,2048]{2,1,0:T(8,128)(2,1)S(1)} %get-tuple-element.76), channel_id=1, source_target_pairs={{0,2},{2,4},{4,6},{6,0},{1,3},{3,5},{5,7},{7,1},{8,10},{10,12},{12... | collective-permute-start | bytes 196616 | tf_op jit(solution)/shard_map/ppermute | solution.py:471
  82.8 11.1 %collective-permute-start.9 = (bf16[2,8,2048]{2,1,0:T(8,128)(2,1)S(1)}, bf16[2,8,2048]{2,1,0:T(8,128)(2,1)S(1)}, u32[]{:S(2)}, u32[]{:S(2)}) collective-permute-start(bf16[2,8,2048]{2,1,0:T(8,128)(2,1)S(1)} %get-tuple-element.75), channel_id=1, source_target_pairs={{0,4},{2,6},{4,0},{6,2},{1,5},{3,7},{5,1},{7,3},{8,12},{10,14},{12... | collective-permute-start | bytes 196616 | tf_op jit(solution)/shard_map/ppermute | solution.py:471
  83.9 9.9 %collective-permute-start.10 = (bf16[2,8,2048]{2,1,0:T(8,128)(2,1)S(1)}, bf16[2,8,2048]{2,1,0:T(8,128)(2,1)S(1)}, u32[]{:S(2)}, u32[]{:S(2)}) collective-permute-start(bf16[2,8,2048]{2,1,0:T(8,128)(2,1)S(1)} %get-tuple-element.74), channel_id=1, source_target_pairs={{0,6},{2,0},{4,2},{6,4},{1,7},{3,1},{5,3},{7,5},{8,14},{10,8},{12,... | collective-permute-start | bytes 196616 | tf_op jit(solution)/shard_map/ppermute | solution.py:471
  88.3 12.4 %copy-start.8 = (bf16[8,8,1024]{2,1,0:T(8,128)(2,1)}, bf16[8,8,1024]{2,1,0:T(8,128)(2,1)S(1)}, u32[]{:S(2)}) copy-start(bf16[8,8,1024]{2,1,0:T(8,128)(2,1)S(1)} %collective-permute-done.12.in_cor) | copy-start | bytes 393220
  88.4 12.4 %collective-permute-start.13 = (bf16[8,32,1024]{2,1,0:T(8,128)(2,1)S(1)}, bf16[8,32,1024]{2,1,0:T(8,128)(2,1)S(1)}, u32[]{:S(2)}, u32[]{:S(2)}) collective-permute-start(bf16[8,32,1024]{2,1,0:T(8,128)(2,1)S(1)} %copy-done.9), channel_id=1, source_target_pairs={{0,8},{1,9},{2,10},{3,11},{4,12},{5,13},{6,14},{7,15},{8,16},{9,17... | collective-permute-start | bytes 1572872 | tf_op jit(solution)/shard_map/ppermute | solution.py:462
  93.9 6.9 %copy-start.5 = (bf16[64,8,512]{2,1,0:T(8,128)(2,1)}, bf16[64,8,512]{2,1,0:T(8,128)(2,1)S(1)}, u32[]{:S(2)}) copy-start(bf16[64,8,512]{2,1,0:T(8,128)(2,1)S(1)} %collective-permute-done.11.in_grad) | copy-start | bytes 1572868
  94.0 11.4 %collective-permute-start.16 = (bf16[4,2048]{1,0:T(4,128)(2,1)S(1)}, bf16[4,2048]{1,0:T(4,128)(2,1)S(1)}, u32[]{:S(2)}, u32[]{:S(2)}) collective-permute-start(bf16[4,2048]{1,0:T(4,128)(2,1)S(1)} %get-tuple-element.79), channel_id=1, source_target_pairs={{0,65},{1,0},{64,1},{65,64},{2,67},{3,2},{66,3},{67,66},{4,69},{5,... | collective-permute-start | bytes 49160 | tf_op jit(solution)/shard_map/ppermute | solution.py:471
  94.2 11.2 %collective-permute-start.15 = (bf16[4,2048]{1,0:T(4,128)(2,1)S(1)}, bf16[4,2048]{1,0:T(4,128)(2,1)S(1)}, u32[]{:S(2)}, u32[]{:S(2)}) collective-permute-start(bf16[4,2048]{1,0:T(4,128)(2,1)S(1)} %get-tuple-element.80), channel_id=1, source_target_pairs={{0,64},{1,65},{64,0},{65,1},{2,66},{3,67},{66,2},{67,3},{4,68},{5,... | collective-permute-start | bytes 49160 | tf_op jit(solution)/shard_map/ppermute | solution.py:471
  97.3 8.1 %collective-permute-start.14 = (bf16[4,2048]{1,0:T(4,128)(2,1)S(1)}, bf16[4,2048]{1,0:T(4,128)(2,1)S(1)}, u32[]{:S(2)}, u32[]{:S(2)}) collective-permute-start(bf16[4,2048]{1,0:T(4,128)(2,1)S(1)} %get-tuple-element.78), channel_id=1, source_target_pairs={{0,1},{1,64},{64,65},{65,0},{2,3},{3,66},{66,67},{67,2},{4,5},{5,6... | collective-permute-start | bytes 49160 | tf_op jit(solution)/shard_map/ppermute | solution.py:471
  100.8 0.8 copy-start.6

commit v2 on v1

--- a/solution.py
+++ b/solution.py
@@ -374,46 +374,39 @@
     wait_all(start_all([(b, a) for a, b in pairs], sems))
 
 
-def place_lat(s1, came, side):
-    mark = iota((8, 8, D), 1) < s1
-
-    def place(r, carry):
-        at = pl.ds(pl.multiple_of(r * 8, 8), 8)
-        rows = side[at, 0:8, :].astype(F32)
-        side[at, 0:8, :] = jnp.where(mark, came[at, :, :].astype(F32), rows).astype(BF)
-        return carry
-
-    lax.fori_loop(0, 8, place, 0)
-
-
-def updated_return_kernel(shifts, updated, in_up, out_updated, side, sems):
-    pairs = [(out_updated.at[:, 0:16, :], side)]
-    wait_all(start_all(pairs, sems))
-    place_lat(shifts[1], in_up, side)
-    wait_all(start_all([(b, a) for a, b in pairs], sems))
-
-
 def return_kernel(
-    shifts, updated, tokens_grad, in_grad, in_lon, in_cor, out_updated, out_grad, side, top, sems
+    shifts, updated, tokens_grad, in_up, in_grad, in_lon, in_cor, out_updated, out_grad, side, top, sems
 ):
     s0, s1 = shifts[0], shifts[1]
-    pairs = [(out_grad.at[8:64, 0:16, :], side.at[8:64])]
-    pairs += [(out.at[0:8], top.at[n]) for n, out in enumerate((out_updated, out_grad))]
-    wait_all(start_all(pairs, sems))
-    place_lat(s1, in_grad, side)
+    outs = (out_updated, out_grad)
+    tops = [(out.at[0:8], top.at[n]) for n, out in enumerate(outs)]
+    sides = [(out.at[8:64, 0:16, :], side.at[n, 8:64]) for n, out in enumerate(outs)]
+    tops_in, sides_in = start_all(tops, sems), start_all(sides, sems, 2)
+    wait_all(tops_in)
     early = iota((8, 32, D), 0) < s0
     first = iota((8, 8, D), 1) < s1
-    for n in range(2):
+    for n, in_lat in enumerate((in_up, in_grad)):
         cols = slice(n * D, n * D + D)
         came = in_lon[:, :, cols].astype(F32)
         corner = jnp.where(first, in_cor[:, :, cols].astype(F32), came[:, 0:8])
         came = jnp.concatenate([corner, came[:, 8:]], axis=1)
         old = top[n].astype(F32)
-        if n == 1:
-            back = jnp.where(first, in_grad[0:8, :, :].astype(F32), old[:, 0:8])
-            old = jnp.concatenate([back, old[:, 8:]], axis=1)
+        back = jnp.where(first, in_lat[0:8, :, :].astype(F32), old[:, 0:8])
+        old = jnp.concatenate([back, old[:, 8:]], axis=1)
         top[n] = jnp.where(early, came, old).astype(BF)
-    wait_all(start_all([(b, a) for a, b in pairs], sems))
+    wait_all(sides_in)
+    copies = start_all([(b, a) for a, b in tops], sems)
+    for n, in_lat in enumerate((in_up, in_grad)):
+
+        def place(r, carry, n=n, in_lat=in_lat):
+            at = pl.ds(pl.multiple_of(r * 8, 8), 8)
+            rows = side[n, at, 0:8, :].astype(F32)
+            side[n, at, 0:8, :] = jnp.where(first, in_lat[at, :, :].astype(F32), rows).astype(BF)
+            return carry
+
+        lax.fori_loop(1, 8, place, 0)
+        copies += start_all([sides[n][::-1]], sems, 2 + n)
+    wait_all(copies)
 
 
 def vmem(shape, dtype):
@@ -531,17 +524,12 @@
     )(*args)
 
 
-def run_updated_return(*args):
-    scratch = [vmem((64, 16, D), BF), DMA((1,))]
-    return call(updated_return_kernel, GRID, scratch, [IN_HBM, IN_VMEM], IN_HBM, {1: 0})(*args)
-
-
 def run_return(*args):
     return call(
         return_kernel,
         [GRID, GRID],
-        [vmem((64, 16, D), BF), vmem((2, 8, 32, D), BF), DMA((3,))],
-        [IN_HBM] * 2 + [IN_VMEM] * 3,
+        [vmem((2, 64, 16, D), BF), vmem((2, 8, 32, D), BF), DMA((4,))],
+        [IN_HBM] * 2 + [IN_VMEM] * 4,
         [IN_HBM] * 2,
         {1: 0, 2: 1},
     )(*args)
@@ -562,8 +550,7 @@
 
     def merge_beside(blocks):
         _, *placed = lax.optimization_barrier((blocks, updated, tokens_grad))
-        placed, grad = run_edge_merge(shifts, *placed, *edges)
-        return run_updated_return(shifts, placed, in_up), grad
+        return *run_edge_merge(shifts, *placed, *edges), in_up
 
     w_got = lax.ppermute(w_other, "core", [(0, 1), (1, 0)])
     in_up = shift_to(out_up, 0, 1)
@@ -572,12 +559,12 @@
     in_cor = shift_to(out_cor, 1, 1)
     total = (w_mine.astype(F32) + w_got.astype(F32)).astype(BF)
     total = total.reshape(2, 4, 32, 4 * D).transpose(1, 0, 2, 3)
-    total, (updated, tokens_grad) = scatter_sum(total, "x", 4, merge_beside)
+    total, (updated, tokens_grad, in_up) = scatter_sum(total, "x", 4, merge_beside)
     total = total.astype(BF).reshape(2, 4, 8, 4 * D).transpose(1, 0, 2, 3)
-    total, (in_grad, in_cor) = scatter_sum(total, "y", 4, lambda blocks: (in_grad, in_cor))
+    total, (in_grad, in_lon) = scatter_sum(total, "y", 4, lambda blocks: (in_grad, in_lon))
     total, _ = scatter_sum(total.astype(BF).reshape(4, 4, 4 * D), ("zh", "zl"), 4)
 
-    updated, tokens_grad = run_return(shifts, updated, tokens_grad, in_grad, in_lon, in_cor)
+    updated, tokens_grad = run_return(shifts, updated, tokens_grad, in_up, in_grad, in_lon, in_cor)
     return (updated, tokens_grad, total[:, : 3 * D], total[:, 3 * D :])
 
 

time: 108 us -> 111 us (1.028); the launches traced: 107 us -> 111 us
  waiting for transfers between devices: 9.43 us -> 22 us
  starting transfers between devices: 28.8 us -> 24.1 us
  Pallas kernels: 60.1 us -> 57.3 us
    ppermute x7, waiting for transfers between devices: 8.47 us -> 17.8 us  [shift_to(): return lax.ppermute(value, ALL, pairs)]
    ppermute x7, starting transfers between devices: 18.8 us -> 13.3 us  [shift_to(): return lax.ppermute(value, ALL, pairs)]
    ppermute x9, waiting for transfers between devices: 0.02 us -> 3.27 us  [scatter_sum(): parts.append(lax.ppermute(block, axes, pairs))]
    pallas_call x2 -> x1, Pallas kernels: 7.24 us -> 4.44 us  [run_return(): call(return_kernel, [GRID, GRID], [vmem((2, 64, 16, D), BF), vmem((2, 8,...]
  transfers between devices with their start and end apart: 17 -> 17, of which waited for: 4 -> 6; matrix products, arithmetic and copies ran while one was open for 2% -> 2% of each run, Pallas kernels for 39% -> 35%
where the time goes in v2:
time: 111 us
  Pallas kernels  57.3 us (52%)
  starting transfers between devices  24.1 us (22%)
  waiting for transfers between devices  22 us (20%)
  local copies, waits for them, and re-layouts  4.44 us (4%)
  other arithmetic  2.01 us (2%)
    pallas_call x1, Pallas kernels, run_interior(): call(interior_kernel, [GRID, GRID, sds((D, 4 * D), F32), sds((32, 128), F...  29.4 us
    pallas_call x1, Pallas kernels, run_edge(): call(edge_kernel, [sds(shape, BF) for shape in (lat, lon, lat, lon, near,...  18.4 us
    ppermute x7, waiting for transfers between devices, shift_to(): return lax.ppermute(value, ALL, pairs)  17.8 us
    ppermute x7, starting transfers between devices, shift_to(): return lax.ppermute(value, ALL, pairs)  13.3 us
    ppermute x9, starting transfers between devices, scatter_sum(): parts.append(lax.ppermute(block, axes, pairs))  10.8 us
    pallas_call x1, Pallas kernels, run_edge_merge(): call(edge_merge_kernel, [GRID, GRID], [vmem((2, 64, 16, D), BF), vmem((2,...  5.1 us
    pallas_call x1, Pallas kernels, run_return(): call(return_kernel, [GRID, GRID], [vmem((2, 64, 16, D), BF), vmem((2, 8,...  4.44 us
    ppermute x9, waiting for transfers between devices, scatter_sum(): parts.append(lax.ppermute(block, axes, pairs))  3.27 us
  transfers between devices with their start and end apart: 17, of which 6 were waited for; matrix products, arithmetic and copies ran while one was open for 2% of the time, Pallas kernels for 35%

profile of v2, /device:TPU:0, one launch (start us, length us, event | category | flops | bytes accessed | tf_op | source)
XLA Modules:
  0.0 110.8 jit_solution(9277060246419134341)
XLA Ops:
  0.7 1.0 slice-done.2
  1.7 0.2 slice-done
  1.8 0.1 pad_maximum_fusion
  2.0 4.5 %collective-permute-start.1 = (bf16[64,8,1024]{2,1,0:T(8,128)(2,1)S(1)}, bf16[64,8,1024]{2,1,0:T(8,128)(2,1)S(1)}, u32[]{:S(2)}, u32[]{:S(2)}) collective-permute-start(bf16[64,8,1024]{2,1,0:T(8,128)(2,1)S(1)} %pad_maximum_fusion), channel_id=1, source_target_pairs={{0,7},{1,0},{2,1},{3,2},{4,3},{5,4},{6,5},{7,6},{8,15},{9,8},{10,9... | collective-permute-start | bytes 3145736 | tf_op jit(solution)/shard_map/ppermute | solution.py:455
  6.6 5.0 %collective-permute-start = (bf16[8,32,1024]{2,1,0:T(8,128)(2,1)S(1)}, bf16[8,32,1024]{2,1,0:T(8,128)(2,1)S(1)}, u32[]{:S(2)}, u32[]{:S(2)}) collective-permute-start(bf16[8,32,1024]{2,1,0:T(8,128)(2,1)S(1)} %pad_maximum_fusion.1), channel_id=1, source_target_pairs={{0,120},{1,121},{2,122},{3,123},{4,124},{5,125},{6,126},{7,127},{8... | collective-permute-start | bytes 1572872 | tf_op jit(solution)/shard_map/ppermute | solution.py:455
  11.6 0.3 collective-permute-start.2
  11.9 29.4 %shard_map.111 = (bf16[64,32,512]{2,1,0:T(8,128)(2,1)}, bf16[64,32,512]{2,1,0:T(8,128)(2,1)}, f32[512,2048]{1,0:T(8,128)}, f32[32,128]{1,0:T(8,128)}, f32[64,512]{1,0:T(8,128)}) custom-call(s32[2]{0:T(128)} %shifts.7, bf16[64,32,512]{2,1,0:T(8,128)(2,1)} %tokens_in.3, bf16[64,32,512]{2,1,0:T(8,128)(2,1)} %grads_in.3, s32[1024,256]{1,0:T(8,128)} %pad_in.1, ...), custom_call_target="tpu_custom_call" | custom-call | tf_op jit(solution)/shard_map/pallas_call | solution.py:485
  41.4 0.6 copy-done.7
  42.0 0.2 copy-done.6
  42.2 0.4 copy-done.2
  42.5 18.4 %shard_map.112 = (bf16[64,16,512]{2,1,0:T(8,128)(2,1)}, bf16[8,32,512]{2,1,0:T(8,128)(2,1)}, bf16[64,16,512]{2,1,0:T(8,128)(2,1)}, bf16[8,32,512]{2,1,0:T(8,128)...) custom-call(s32[2]{0:T(128)} %shifts.7, ...), custom_call_target="tpu_custom_call" | custom-call | tf_op jit(solution)/shard_map/pallas_call | solution.py:500
  61.1 1.9 %collective-permute-start.7 = (bf16[64,8,512]{2,1,0:T(8,128)(2,1)}, bf16[64,8,512]{2,1,0:T(8,128)(2,1)S(1)}, u32[]{:S(2)}, u32[]{:S(2)}) collective-permute-start(bf16[64,8,512]{2,1,0:T(8,128)(2,1)} %get-tuple-element.53), channel_id=1, source_target_pairs={{0,1},{1,2},{2,3},{3,4},{4,5},{5,6},{6,7},{7,0},{8,9},{9,10},{10,1... | collective-permute-start | bytes 1572872 | tf_op jit(solution)/shard_map/ppermute | solution.py:455
  62.9 0.9 collective-permute-done.3
  63.9 1.6 %add_convert_fusion = bf16[256,2048]{1,0:T(8,128)(2,1)S(1)} fusion(bf16[256,2048]{1,0:T(8,128)(2,1)S(1)} %collective-permute-done.3, bf16[256,2048]{1,0:T(8,128)(2,1)} %get-tuple-element.41), kind=kLoop, calls=%fused_computation | loop fusion | flops 2097152 | bytes 3145728 | tf_op jit(solution)/shard_map/convert_element_type | solution.py:560
  65.7 0.2 collective-permute-start.5
  65.9 3.0 %collective-permute-start.6 = (bf16[2,32,2048]{2,1,0:T(8,128)(2,1)S(1)}, bf16[2,32,2048]{2,1,0:T(8,128)(2,1)S(1)}, u32[]{:S(2)}, u32[]{:S(2)}) collective-permute-start(bf16[2,32,2048]{2,1,0:T(8,128)(2,1)S(1)} %get-tuple-element.72), channel_id=1, source_target_pairs={{0,48},{16,0},{32,16},{48,32},{1,49},{17,1},{33,17},{49,33},{2,50}... | collective-permute-start | bytes 786440 | tf_op jit(solution)/shard_map/ppermute | solution.py:464
  68.9 1.6 %collective-permute-start.11 = (bf16[64,8,512]{2,1,0:T(8,128)(2,1)}, bf16[64,8,512]{2,1,0:T(8,128)(2,1)S(1)}, u32[]{:S(2)}, u32[]{:S(2)}) collective-permute-start(bf16[64,8,512]{2,1,0:T(8,128)(2,1)} %get-tuple-element.61), channel_id=1, source_target_pairs={{0,1},{1,2},{2,3},{3,4},{4,5},{5,6},{6,7},{7,0},{8,9},{9,10},{10,1... | collective-permute-start | bytes 1572872 | tf_op jit(solution)/shard_map/ppermute | solution.py:455
  70.5 5.1 %shard_map.113 = (bf16[64,32,512]{2,1,0:T(8,128)(2,1)}, bf16[64,32,512]{2,1,0:T(8,128)(2,1)}) custom-call(s32[2]{0:T(128)} %shifts.7, bf16[64,32,512]{2,1,0:T(8,128)(2,1)} %get-tuple-element.45.updated, bf16[64,32,512]{2,1,0:T(8,128)(2,1)} %get-tuple-element.46.tokens_grad, ...), custom_call_target="tpu_custom_call", output_to_operand_aliasing={{0}: (1, {}), {1}: (2, {})} | custom-call | tf_op jit(solution)/shard_map/pallas_call | solution.py:517
  75.6 2.6 %collective-permute-done.7.in_up = bf16[64,8,512]{2,1,0:T(8,128)(2,1)S(1)} collective-permute-done((bf16[64,8,512]{2,1,0:T(8,128)(2,1)}, bf16[64,8,512]{2,1,0:T(8,128)(2,1)S(1)}, u32[]{:S(2)}, u32[]{:S(2)}) %collective-permute-start.7) | collective-permute-done | bytes 524320 | tf_op jit(solution)/shard_map/ppermute | solution.py:455
  78.2 2.6 %collective-permute-done.4 = bf16[2,32,2048]{2,1,0:T(8,128)(2,1)S(1)} collective-permute-done((bf16[2,32,2048]{2,1,0:T(8,128)(2,1)S(1)}, bf16[2,32,2048]{2,1,0:T(8,128)(2,1)S(1)}, u32[]{:S(2)}, u32[]{:S(2)}) %collective-permute-start.4) | collective-permute-done | bytes 262176 | tf_op jit(solution)/shard_map/ppermute | solution.py:464
  80.9 0.6 collective-permute-done.6
  81.5 0.1 fusion
  81.7 2.2 %collective-permute-start.9 = (bf16[2,8,2048]{2,1,0:T(8,128)(2,1)S(1)}, bf16[2,8,2048]{2,1,0:T(8,128)(2,1)S(1)}, u32[]{:S(2)}, u32[]{:S(2)}) collective-permute-start(bf16[2,8,2048]{2,1,0:T(8,128)(2,1)S(1)} %get-tuple-element.77), channel_id=1, source_target_pairs={{0,4},{2,6},{4,0},{6,2},{1,5},{3,7},{5,1},{7,3},{8,12},{10,14},{12... | collective-permute-start | bytes 196616 | tf_op jit(solution)/shard_map/ppermute | solution.py:464
  83.9 1.1 collective-permute-start.10
  85.0 9.5 %collective-permute-done.11.in_grad = bf16[64,8,512]{2,1,0:T(8,128)(2,1)S(1)} collective-permute-done((bf16[64,8,512]{2,1,0:T(8,128)(2,1)}, bf16[64,8,512]{2,1,0:T(8,128)(2,1)S(1)}, u32[]{:S(2)}, u32[]{:S(2)}) %collective-permute-start.11) | collective-permute-done | bytes 524320 | tf_op jit(solution)/shard_map/ppermute | solution.py:455
  94.7 1.5 %collective-permute-start.16 = (bf16[4,2048]{1,0:T(4,128)(2,1)S(1)}, bf16[4,2048]{1,0:T(4,128)(2,1)S(1)}, u32[]{:S(2)}, u32[]{:S(2)}) collective-permute-start(bf16[4,2048]{1,0:T(4,128)(2,1)S(1)} %get-tuple-element.81), channel_id=1, source_target_pairs={{0,65},{1,0},{64,1},{65,64},{2,67},{3,2},{66,3},{67,66},{4,69},{5,... | collective-permute-start | bytes 49160 | tf_op jit(solution)/shard_map/ppermute | solution.py:464
  96.2 2.6 %collective-permute-start.15 = (bf16[4,2048]{1,0:T(4,128)(2,1)S(1)}, bf16[4,2048]{1,0:T(4,128)(2,1)S(1)}, u32[]{:S(2)}, u32[]{:S(2)}) collective-permute-start(bf16[4,2048]{1,0:T(4,128)(2,1)S(1)} %get-tuple-element.82), channel_id=1, source_target_pairs={{0,64},{1,65},{64,0},{65,1},{2,66},{3,67},{66,2},{67,3},{4,68},{5,... | collective-permute-start | bytes 49160 | tf_op jit(solution)/shard_map/ppermute | solution.py:464
  98.8 5.6 %collective-permute-done.13.in_cor = bf16[8,8,1024]{2,1,0:T(8,128)(2,1)S(1)} collective-permute-done((bf16[8,8,1024]{2,1,0:T(8,128)(2,1)S(1)}, bf16[8,8,1024]{2,1,0:T(8,128)(2,1)S(1)}, u32[]{:S(2)}, u32[]{:S(2)}) %collective-permute-start.13) | collective-permute-done | bytes 131104 | tf_op jit(solution)/shard_map/ppermute | solution.py:455
  104.4 0.6 copy-done.8
  105.1 4.4 %shard_map.114 = (bf16[64,32,512]{2,1,0:T(8,128)(2,1)}, bf16[64,32,512]{2,1,0:T(8,128)(2,1)}) custom-call(s32[2]{0:T(128)} %shifts.7, bf16[64,32,512]{2,1,0:T(8,128)(2,1)} %get-tuple-element.54.updated, bf16[64,32,512]{2,1,0:T(8,128)(2,1)} %get-tuple-element.55.tokens_grad, ...), custom_call_target="tpu_custom_call", output_to_operand_aliasing={{0}: (1, {}), {1}: (2, {})} | custom-call | tf_op jit(solution)/shard_map/pallas_call | solution.py:528
  109.6 0.6 slice.32
  110.2 0.6 slice.33
  (49 shorter events, 0.7 us)
Async XLA Ops:
  0.6 1.0 slice-start.2
  0.6 1.2 %slice-start = ((bf16[64,32,512]{2,1,0:T(8,128)(2,1)}), bf16[64,8,512]{2,1,0:T(8,128)(2,1)S(1)}, s32[]{:S(2)}) async-start(bf16[64,32,512]{2,1,0:T(8,128)(2,1)} %tokens_in.3), calls=%async_computation | async-start | bytes 1048576 | tf_op jit(solution)/shard_map/slice | solution.py:539
  0.7 5.9 %slice-start.1 = ((bf16[64,32,512]{2,1,0:T(8,128)(2,1)}), bf16[8,32,512]{2,1,0:T(8,128)(2,1)S(1)}, s32[]{:S(2)}) async-start(bf16[64,32,512]{2,1,0:T(8,128)(2,1)} %tokens_in.3), calls=%async_computation.1 | async-start | bytes 524288 | tf_op jit(solution)/shard_map/slice | solution.py:539
  0.7 5.8 %slice-start.3 = ((bf16[64,32,512]{2,1,0:T(8,128)(2,1)}), bf16[8,32,512]{2,1,0:T(8,128)(2,1)S(1)}, s32[]{:S(2)}) async-start(bf16[64,32,512]{2,1,0:T(8,128)(2,1)} %grads_in.3), calls=%async_computation.3 | async-start | bytes 524288 | tf_op jit(solution)/shard_map/slice | solution.py:539
  0.7 10.9 %copy-start.1 = (bf16[64,32,512]{2,1,0:T(8,128)(2,1)S(1)}, bf16[64,32,512]{2,1,0:T(8,128)(2,1)}, u32[]{:S(2)}) copy-start(bf16[64,32,512]{2,1,0:T(8,128)(2,1)} %grads_in.3) | copy-start | bytes 6291460
  1.8 9.8 %copy-start = (bf16[64,32,512]{2,1,0:T(8,128)(2,1)S(1)}, bf16[64,32,512]{2,1,0:T(8,128)(2,1)}, u32[]{:S(2)}) copy-start(bf16[64,32,512]{2,1,0:T(8,128)(2,1)} %tokens_in.3) | copy-start | bytes 6291460
  2.0 39.4 %collective-permute-start.1 = (bf16[64,8,1024]{2,1,0:T(8,128)(2,1)S(1)}, bf16[64,8,1024]{2,1,0:T(8,128)(2,1)S(1)}, u32[]{:S(2)}, u32[]{:S(2)}) collective-permute-start(bf16[64,8,1024]{2,1,0:T(8,128)(2,1)S(1)} %pad_maximum_fusion), channel_id=1, source_target_pairs={{0,7},{1,0},{2,1},{3,2},{4,3},{5,4},{6,5},{7,6},{8,15},{9,8},{10,9... | collective-permute-start | bytes 3145736 | tf_op jit(solution)/shard_map/ppermute | solution.py:455
  6.6 34.8 %collective-permute-start = (bf16[8,32,1024]{2,1,0:T(8,128)(2,1)S(1)}, bf16[8,32,1024]{2,1,0:T(8,128)(2,1)S(1)}, u32[]{:S(2)}, u32[]{:S(2)}) collective-permute-start(bf16[8,32,1024]{2,1,0:T(8,128)(2,1)S(1)} %pad_maximum_fusion.1), channel_id=1, source_target_pairs={{0,120},{1,121},{2,122},{3,123},{4,124},{5,125},{6,126},{7,127},{8... | collective-permute-start | bytes 1572872 | tf_op jit(solution)/shard_map/ppermute | solution.py:455
  11.6 29.7 %collective-permute-start.2 = (bf16[8,8,1024]{2,1,0:T(8,128)(2,1)S(1)}, bf16[8,8,1024]{2,1,0:T(8,128)(2,1)S(1)}, u32[]{:S(2)}, u32[]{:S(2)}) collective-permute-start(bf16[8,8,1024]{2,1,0:T(8,128)(2,1)S(1)} %pad_maximum_fusion.2), channel_id=1, source_target_pairs={{0,127},{1,120},{2,121},{3,122},{4,123},{5,124},{6,125},{7,126},{8... | collective-permute-start | bytes 393224 | tf_op jit(solution)/shard_map/ppermute | solution.py:455
  41.3 0.7 copy-start.7
  41.3 0.8 copy-start.6
  41.4 1.2 %copy-start.2 = (bf16[64,8,1024]{2,1,0:T(8,128)(2,1)}, bf16[64,8,1024]{2,1,0:T(8,128)(2,1)S(1)}, u32[]{:S(2)}) copy-start(bf16[64,8,1024]{2,1,0:T(8,128)(2,1)S(1)} %collective-permute-done.1.halo_lat) | copy-start | bytes 3145732
  60.9 3.0 %collective-permute-start.3 = (bf16[256,2048]{1,0:T(8,128)(2,1)}, bf16[256,2048]{1,0:T(8,128)(2,1)S(1)}, u32[]{:S(2)}, u32[]{:S(2)}) collective-permute-start(bf16[256,2048]{1,0:T(8,128)(2,1)} %get-tuple-element.42), channel_id=1, source_target_pairs={{0,8},{8,0},{1,9},{9,1},{2,10},{10,2},{3,11},{11,3},{4,12},{12,4},... | collective-permute-start | bytes 3145736 | tf_op jit(solution)/shard_map/ppermute | solution.py:555
  61.1 17.1 %collective-permute-start.7 = (bf16[64,8,512]{2,1,0:T(8,128)(2,1)}, bf16[64,8,512]{2,1,0:T(8,128)(2,1)S(1)}, u32[]{:S(2)}, u32[]{:S(2)}) collective-permute-start(bf16[64,8,512]{2,1,0:T(8,128)(2,1)} %get-tuple-element.53), channel_id=1, source_target_pairs={{0,1},{1,2},{2,3},{3,4},{4,5},{5,6},{6,7},{7,0},{8,9},{9,10},{10,1... | collective-permute-start | bytes 1572872 | tf_op jit(solution)/shard_map/ppermute | solution.py:455
  65.6 15.2 %collective-permute-start.4 = (bf16[2,32,2048]{2,1,0:T(8,128)(2,1)S(1)}, bf16[2,32,2048]{2,1,0:T(8,128)(2,1)S(1)}, u32[]{:S(2)}, u32[]{:S(2)}) collective-permute-start(bf16[2,32,2048]{2,1,0:T(8,128)(2,1)S(1)} %get-tuple-element.74), channel_id=1, source_target_pairs={{0,16},{16,32},{32,48},{48,0},{1,17},{17,33},{33,49},{49,1},{2,18}... | collective-permute-start | bytes 786440 | tf_op jit(solution)/shard_map/ppermute | solution.py:464
  65.7 15.2 %collective-permute-start.5 = (bf16[2,32,2048]{2,1,0:T(8,128)(2,1)S(1)}, bf16[2,32,2048]{2,1,0:T(8,128)(2,1)S(1)}, u32[]{:S(2)}, u32[]{:S(2)}) collective-permute-start(bf16[2,32,2048]{2,1,0:T(8,128)(2,1)S(1)} %get-tuple-element.73), channel_id=1, source_target_pairs={{0,32},{16,48},{32,0},{48,16},{1,33},{17,49},{33,1},{49,17},{2,34}... | collective-permute-start | bytes 786440 | tf_op jit(solution)/shard_map/ppermute | solution.py:464
  65.9 15.6 %collective-permute-start.6 = (bf16[2,32,2048]{2,1,0:T(8,128)(2,1)S(1)}, bf16[2,32,2048]{2,1,0:T(8,128)(2,1)S(1)}, u32[]{:S(2)}, u32[]{:S(2)}) collective-permute-start(bf16[2,32,2048]{2,1,0:T(8,128)(2,1)S(1)} %get-tuple-element.72), channel_id=1, source_target_pairs={{0,48},{16,0},{32,16},{48,32},{1,49},{17,1},{33,17},{49,33},{2,50}... | collective-permute-start | bytes 786440 | tf_op jit(solution)/shard_map/ppermute | solution.py:464
  68.9 25.6 %collective-permute-start.11 = (bf16[64,8,512]{2,1,0:T(8,128)(2,1)}, bf16[64,8,512]{2,1,0:T(8,128)(2,1)S(1)}, u32[]{:S(2)}, u32[]{:S(2)}) collective-permute-start(bf16[64,8,512]{2,1,0:T(8,128)(2,1)} %get-tuple-element.61), channel_id=1, source_target_pairs={{0,1},{1,2},{2,3},{3,4},{4,5},{5,6},{6,7},{7,0},{8,9},{9,10},{10,1... | collective-permute-start | bytes 1572872 | tf_op jit(solution)/shard_map/ppermute | solution.py:455
  70.5 24.0 %copy-start.9 = (bf16[8,8,1024]{2,1,0:T(8,128)(2,1)S(1)}, bf16[8,8,1024]{2,1,0:T(8,128)(2,1)}, u32[]{:S(2)}) copy-start(bf16[8,8,1024]{2,1,0:T(8,128)(2,1)} %get-tuple-element.65) | copy-start | bytes 393220
  78.2 26.2 %copy-start.3 = (bf16[64,8,512]{2,1,0:T(8,128)(2,1)}, bf16[64,8,512]{2,1,0:T(8,128)(2,1)S(1)}, u32[]{:S(2)}) copy-start(bf16[64,8,512]{2,1,0:T(8,128)(2,1)S(1)} %collective-permute-done.7.in_up) | copy-start | bytes 1572868
  78.2 16.3 %collective-permute-start.12 = (bf16[8,32,1024]{2,1,0:T(8,128)(2,1)}, bf16[8,32,1024]{2,1,0:T(8,128)(2,1)S(1)}, u32[]{:S(2)}, u32[]{:S(2)}) collective-permute-start(bf16[8,32,1024]{2,1,0:T(8,128)(2,1)} %get-tuple-element.62), channel_id=1, source_target_pairs={{0,8},{1,9},{2,10},{3,11},{4,12},{5,13},{6,14},{7,15},{8,16},{9,17... | collective-permute-start | bytes 1572872 | tf_op jit(solution)/shard_map/ppermute | solution.py:455
  81.7 12.9 %collective-permute-start.8 = (bf16[2,8,2048]{2,1,0:T(8,128)(2,1)S(1)}, bf16[2,8,2048]{2,1,0:T(8,128)(2,1)S(1)}, u32[]{:S(2)}, u32[]{:S(2)}) collective-permute-start(bf16[2,8,2048]{2,1,0:T(8,128)(2,1)S(1)} %get-tuple-element.78), channel_id=1, source_target_pairs={{0,2},{2,4},{4,6},{6,0},{1,3},{3,5},{5,7},{7,1},{8,10},{10,12},{12... | collective-permute-start | bytes 196616 | tf_op jit(solution)/shard_map/ppermute | solution.py:464
  81.7 12.8 %collective-permute-start.9 = (bf16[2,8,2048]{2,1,0:T(8,128)(2,1)S(1)}, bf16[2,8,2048]{2,1,0:T(8,128)(2,1)S(1)}, u32[]{:S(2)}, u32[]{:S(2)}) collective-permute-start(bf16[2,8,2048]{2,1,0:T(8,128)(2,1)S(1)} %get-tuple-element.77), channel_id=1, source_target_pairs={{0,4},{2,6},{4,0},{6,2},{1,5},{3,7},{5,1},{7,3},{8,12},{10,14},{12... | collective-permute-start | bytes 196616 | tf_op jit(solution)/shard_map/ppermute | solution.py:464
  83.9 10.6 %collective-permute-start.10 = (bf16[2,8,2048]{2,1,0:T(8,128)(2,1)S(1)}, bf16[2,8,2048]{2,1,0:T(8,128)(2,1)S(1)}, u32[]{:S(2)}, u32[]{:S(2)}) collective-permute-start(bf16[2,8,2048]{2,1,0:T(8,128)(2,1)S(1)} %get-tuple-element.76), channel_id=1, source_target_pairs={{0,6},{2,0},{4,2},{6,4},{1,7},{3,1},{5,3},{7,5},{8,14},{10,8},{12,... | collective-permute-start | bytes 196616 | tf_op jit(solution)/shard_map/ppermute | solution.py:464
  94.5 9.9 %copy-start.4 = (bf16[64,8,512]{2,1,0:T(8,128)(2,1)}, bf16[64,8,512]{2,1,0:T(8,128)(2,1)S(1)}, u32[]{:S(2)}) copy-start(bf16[64,8,512]{2,1,0:T(8,128)(2,1)S(1)} %collective-permute-done.11.in_grad) | copy-start | bytes 1572868
  94.5 9.9 %collective-permute-start.13 = (bf16[8,8,1024]{2,1,0:T(8,128)(2,1)S(1)}, bf16[8,8,1024]{2,1,0:T(8,128)(2,1)S(1)}, u32[]{:S(2)}, u32[]{:S(2)}) collective-permute-start(bf16[8,8,1024]{2,1,0:T(8,128)(2,1)S(1)} %copy-done.9), channel_id=1, source_target_pairs={{0,9},{1,10},{2,11},{3,12},{4,13},{5,14},{6,15},{7,8},{8,17},{9,18... | collective-permute-start | bytes 393224 | tf_op jit(solution)/shard_map/ppermute | solution.py:455
  94.5 9.9 %copy-start.5 = (bf16[8,32,1024]{2,1,0:T(8,128)(2,1)}, bf16[8,32,1024]{2,1,0:T(8,128)(2,1)S(1)}, u32[]{:S(2)}) copy-start(bf16[8,32,1024]{2,1,0:T(8,128)(2,1)S(1)} %collective-permute-done.12.in_lon) | copy-start | bytes 1572868
  94.7 14.8 %collective-permute-start.16 = (bf16[4,2048]{1,0:T(4,128)(2,1)S(1)}, bf16[4,2048]{1,0:T(4,128)(2,1)S(1)}, u32[]{:S(2)}, u32[]{:S(2)}) collective-permute-start(bf16[4,2048]{1,0:T(4,128)(2,1)S(1)} %get-tuple-element.81), channel_id=1, source_target_pairs={{0,65},{1,0},{64,1},{65,64},{2,67},{3,2},{66,3},{67,66},{4,69},{5,... | collective-permute-start | bytes 49160 | tf_op jit(solution)/shard_map/ppermute | solution.py:464
  96.2 13.3 %collective-permute-start.15 = (bf16[4,2048]{1,0:T(4,128)(2,1)S(1)}, bf16[4,2048]{1,0:T(4,128)(2,1)S(1)}, u32[]{:S(2)}, u32[]{:S(2)}) collective-permute-start(bf16[4,2048]{1,0:T(4,128)(2,1)S(1)} %get-tuple-element.82), channel_id=1, source_target_pairs={{0,64},{1,65},{64,0},{65,1},{2,66},{3,67},{66,2},{67,3},{4,68},{5,... | collective-permute-start | bytes 49160 | tf_op jit(solution)/shard_map/ppermute | solution.py:464
  98.8 10.7 %collective-permute-start.14 = (bf16[4,2048]{1,0:T(4,128)(2,1)S(1)}, bf16[4,2048]{1,0:T(4,128)(2,1)S(1)}, u32[]{:S(2)}, u32[]{:S(2)}) collective-permute-start(bf16[4,2048]{1,0:T(4,128)(2,1)S(1)} %get-tuple-element.80), channel_id=1, source_target_pairs={{0,1},{1,64},{64,65},{65,0},{2,3},{3,66},{66,67},{67,2},{4,5},{5,6... | collective-permute-start | bytes 49160 | tf_op jit(solution)/shard_map/ppermute | solution.py:464
  104.4 0.7 copy-start.8

commit v3 on v2

--- a/solution.py
+++ b/solution.py
@@ -243,7 +243,7 @@
 
 def edge_kernel(
     shifts, tokens_in, grads_in, halo_lon, halo_lat, halo_cor, keys, bias, w_qkv_in, w_out_in, w_part,
-    lat_up, lon_up, lat_grad, lon_grad, out_up, out_grad, out_lon, out_cor, w_mine, w_other,
+    lat_up, lon_up, lat_grad, lon_grad, out_lat, out_lon, out_cor, w_mine, w_other,
     tok, grad, far, low_tok, low_grad, low_far, w_qkv, w_out, to_lat, to_lon,
     xt, xg, hid, istd, qkvg, mix, dq, ones, w_sum, sems,
 ):
@@ -324,8 +324,7 @@
             (grad, lat_grad),
             (low_tok.at[0:8], lon_up),
             (low_grad.at[0:8], lon_grad),
-            (to_lat.at[0:64, :, 0:D], out_up),
-            (to_lat.at[0:64, :, D : 2 * D], out_grad),
+            (to_lat.at[0:64], out_lat),
             (to_lat.at[64:72], out_cor),
             (to_lon, out_lon),
         ],
@@ -375,7 +374,7 @@
 
 
 def return_kernel(
-    shifts, updated, tokens_grad, in_up, in_grad, in_lon, in_cor, out_updated, out_grad, side, top, sems
+    shifts, updated, tokens_grad, in_lat, in_lon, in_cor, out_updated, out_grad, side, top, sems
 ):
     s0, s1 = shifts[0], shifts[1]
     outs = (out_updated, out_grad)
@@ -385,23 +384,23 @@
     wait_all(tops_in)
     early = iota((8, 32, D), 0) < s0
     first = iota((8, 8, D), 1) < s1
-    for n, in_lat in enumerate((in_up, in_grad)):
+    for n in range(2):
         cols = slice(n * D, n * D + D)
         came = in_lon[:, :, cols].astype(F32)
         corner = jnp.where(first, in_cor[:, :, cols].astype(F32), came[:, 0:8])
         came = jnp.concatenate([corner, came[:, 8:]], axis=1)
         old = top[n].astype(F32)
-        back = jnp.where(first, in_lat[0:8, :, :].astype(F32), old[:, 0:8])
+        back = jnp.where(first, in_lat[0:8, :, cols].astype(F32), old[:, 0:8])
         old = jnp.concatenate([back, old[:, 8:]], axis=1)
         top[n] = jnp.where(early, came, old).astype(BF)
     wait_all(sides_in)
     copies = start_all([(b, a) for a, b in tops], sems)
-    for n, in_lat in enumerate((in_up, in_grad)):
-
-        def place(r, carry, n=n, in_lat=in_lat):
+    for n in range(2):
+
+        def place(r, carry, n=n):
             at = pl.ds(pl.multiple_of(r * 8, 8), 8)
             rows = side[n, at, 0:8, :].astype(F32)
-            side[n, at, 0:8, :] = jnp.where(first, in_lat[at, :, :].astype(F32), rows).astype(BF)
+            side[n, at, 0:8, :] = jnp.where(first, in_lat[at, :, n * D : n * D + D].astype(F32), rows).astype(BF)
             return carry
 
         lax.fori_loop(1, 8, place, 0)
@@ -496,10 +495,10 @@
 
 def run_edge(*args):
     lat, lon = (64, 16, D), (8, 32, D)
-    near, far_lat, far_lon = (64, 8, D), (64, 8, 2 * D), (8, 32, 2 * D)
+    far_lat, far_lon = (64, 8, 2 * D), (8, 32, 2 * D)
     return call(
         edge_kernel,
-        [sds(shape, BF) for shape in (lat, lon, lat, lon, near, near, far_lon, (8, 8, 2 * D))]
+        [sds(shape, BF) for shape in (lat, lon, lat, lon, far_lat, far_lon, (8, 8, 2 * D))]
         + [sds((D // 2, 4 * D), BF)] * 2,
         [vmem(lat, BF), vmem(lat, BF), vmem(far_lat, BF)]
         + [vmem((16, 32, D), BF), vmem((16, 32, D), BF), vmem((16, 8, 2 * D), BF)]
@@ -509,7 +508,7 @@
         + attend_scratch(OUTER)
         + [vmem((D, 4 * D), F32), DMA((12,))],
         [IN_HBM] * 5 + [IN_VMEM] * 2 + [IN_HBM] * 3,
-        [IN_HBM] * 8 + [IN_VMEM] * 2,
+        [IN_HBM] * 7 + [IN_VMEM] * 2,
     )(*args)
 
 
@@ -529,7 +528,7 @@
         return_kernel,
         [GRID, GRID],
         [vmem((2, 64, 16, D), BF), vmem((2, 8, 32, D), BF), DMA((4,))],
-        [IN_HBM] * 2 + [IN_VMEM] * 4,
+        [IN_HBM] * 2 + [IN_VMEM] * 3,
         [IN_HBM] * 2,
         {1: 0, 2: 1},
     )(*args)
@@ -544,27 +543,26 @@
     updated, tokens_grad, w_part, keys, bias = run_interior(
         shifts, tokens, grad_out, pad_mask, bias_table, rel_index, w_qkv, w_out
     )
-    *edges, out_up, out_grad, out_lon, out_cor, w_mine, w_other = run_edge(
+    *edges, out_lat, out_lon, out_cor, w_mine, w_other = run_edge(
         shifts, tokens, grad_out, halo_lon, halo_lat, halo_cor, keys, bias, w_qkv, w_out, w_part
     )
 
     def merge_beside(blocks):
         _, *placed = lax.optimization_barrier((blocks, updated, tokens_grad))
-        return *run_edge_merge(shifts, *placed, *edges), in_up
+        return *run_edge_merge(shifts, *placed, *edges), in_cor
 
     w_got = lax.ppermute(w_other, "core", [(0, 1), (1, 0)])
-    in_up = shift_to(out_up, 0, 1)
-    in_grad = shift_to(out_grad, 0, 1)
+    in_lat = shift_to(out_lat, 0, 1)
     in_lon = shift_to(out_lon, 1, 0)
     in_cor = shift_to(out_cor, 1, 1)
     total = (w_mine.astype(F32) + w_got.astype(F32)).astype(BF)
     total = total.reshape(2, 4, 32, 4 * D).transpose(1, 0, 2, 3)
-    total, (updated, tokens_grad, in_up) = scatter_sum(total, "x", 4, merge_beside)
+    total, (updated, tokens_grad, in_cor) = scatter_sum(total, "x", 4, merge_beside)
     total = total.astype(BF).reshape(2, 4, 8, 4 * D).transpose(1, 0, 2, 3)
-    total, (in_grad, in_lon) = scatter_sum(total, "y", 4, lambda blocks: (in_grad, in_lon))
+    total, (in_lat, in_lon) = scatter_sum(total, "y", 4, lambda blocks: (in_lat, in_lon))
     total, _ = scatter_sum(total.astype(BF).reshape(4, 4, 4 * D), ("zh", "zl"), 4)
 
-    updated, tokens_grad = run_return(shifts, updated, tokens_grad, in_up, in_grad, in_lon, in_cor)
+    updated, tokens_grad = run_return(shifts, updated, tokens_grad, in_lat, in_lon, in_cor)
     return (updated, tokens_grad, total[:, : 3 * D], total[:, 3 * D :])
 
 

time: 111 us -> 110 us (level)
  starting transfers between devices: 24.1 us -> 27.3 us
  waiting for transfers between devices: 22 us -> 18.8 us
    ppermute x7 -> x6, starting transfers between devices: 13.3 us -> 16.8 us  [shift_to(): return lax.ppermute(value, ALL, pairs)]
    ppermute x9, waiting for transfers between devices: 3.27 us -> 0.47 us  [scatter_sum(): parts.append(lax.ppermute(block, axes, pairs))]
    ppermute x7 -> x6, waiting for transfers between devices: 17.8 us -> 17.4 us  [shift_to(): return lax.ppermute(value, ALL, pairs)]
  transfers between devices with their start and end apart: 17 -> 16, of which waited for: 6 -> 4; matrix products, arithmetic and copies ran while one was open for 2% -> 2% of each run, Pallas kernels for 35% -> 35%
where the time goes in v3:
time: 110 us
  Pallas kernels  57.3 us (52%)
  starting transfers between devices  27.3 us (25%)
  waiting for transfers between devices  18.8 us (17%)
  local copies, waits for them, and re-layouts  3.78 us (3%)
  other arithmetic  2.01 us (2%)
    pallas_call x1, Pallas kernels, run_interior(): call(interior_kernel, [GRID, GRID, sds((D, 4 * D), F32), sds((32, 128), F...  29.4 us
    pallas_call x1, Pallas kernels, run_edge(): call(edge_kernel, [sds(shape, BF) for shape in (lat, lon, lat, lon, far_l...  18.4 us
    ppermute x6, waiting for transfers between devices, shift_to(): return lax.ppermute(value, ALL, pairs)  17.4 us
    ppermute x6, starting transfers between devices, shift_to(): return lax.ppermute(value, ALL, pairs)  16.8 us
    ppermute x9, starting transfers between devices, scatter_sum(): parts.append(lax.ppermute(block, axes, pairs))  10.4 us
    pallas_call x1, Pallas kernels, run_edge_merge(): call(edge_merge_kernel, [GRID, GRID], [vmem((2, 64, 16, D), BF), vmem((2,...  5.06 us
    pallas_call x1, Pallas kernels, run_return(): call(return_kernel, [GRID, GRID], [vmem((2, 64, 16, D), BF), vmem((2, 8,...  4.45 us
  transfers between devices with their start and end apart: 16, of which 4 were waited for; matrix products, arithmetic and copies ran while one was open for 2% of the time, Pallas kernels for 35%

profile of v3, /device:TPU:0, one launch (start us, length us, event | category | flops | bytes accessed | tf_op | source)
XLA Modules:
  0.0 110.1 jit_solution(14600661811641733440)
XLA Ops:
  0.7 1.0 slice-done.2
  1.7 0.2 slice-done
  1.8 0.1 pad_maximum_fusion
  2.0 4.5 %collective-permute-start.1 = (bf16[64,8,1024]{2,1,0:T(8,128)(2,1)S(1)}, bf16[64,8,1024]{2,1,0:T(8,128)(2,1)S(1)}, u32[]{:S(2)}, u32[]{:S(2)}) collective-permute-start(bf16[64,8,1024]{2,1,0:T(8,128)(2,1)S(1)} %pad_maximum_fusion), channel_id=1, source_target_pairs={{0,7},{1,0},{2,1},{3,2},{4,3},{5,4},{6,5},{7,6},{8,15},{9,8},{10,9... | collective-permute-start | bytes 3145736 | tf_op jit(solution)/shard_map/ppermute | solution.py:454
  6.6 5.0 %collective-permute-start = (bf16[8,32,1024]{2,1,0:T(8,128)(2,1)S(1)}, bf16[8,32,1024]{2,1,0:T(8,128)(2,1)S(1)}, u32[]{:S(2)}, u32[]{:S(2)}) collective-permute-start(bf16[8,32,1024]{2,1,0:T(8,128)(2,1)S(1)} %pad_maximum_fusion.1), channel_id=1, source_target_pairs={{0,120},{1,121},{2,122},{3,123},{4,124},{5,125},{6,126},{7,127},{8... | collective-permute-start | bytes 1572872 | tf_op jit(solution)/shard_map/ppermute | solution.py:454
  11.6 0.3 collective-permute-start.2
  11.9 29.4 %shard_map.111 = (bf16[64,32,512]{2,1,0:T(8,128)(2,1)}, bf16[64,32,512]{2,1,0:T(8,128)(2,1)}, f32[512,2048]{1,0:T(8,128)}, f32[32,128]{1,0:T(8,128)}, f32[64,512]{1,0:T(8,128)}) custom-call(s32[2]{0:T(128)} %shifts.7, bf16[64,32,512]{2,1,0:T(8,128)(2,1)} %tokens_in.3, bf16[64,32,512]{2,1,0:T(8,128)(2,1)} %grads_in.3, s32[1024,256]{1,0:T(8,128)} %pad_in.1, ...), custom_call_target="tpu_custom_call" | custom-call | tf_op jit(solution)/shard_map/pallas_call | solution.py:484
  41.4 0.6 copy-done.6
  42.0 0.2 copy-done.5
  42.2 0.4 copy-done.2
  42.5 18.4 %shard_map.112 = (bf16[64,16,512]{2,1,0:T(8,128)(2,1)}, bf16[8,32,512]{2,1,0:T(8,128)(2,1)}, bf16[64,16,512]{2,1,0:T(8,128)(2,1)}, bf16[8,32,512]{2,1,0:T(8,128)...) custom-call(s32[2]{0:T(128)} %shifts.7, ...), custom_call_target="tpu_custom_call" | custom-call | tf_op jit(solution)/shard_map/pallas_call | solution.py:499
  60.9 0.1 collective-permute-start.3
  61.0 1.9 %collective-permute-start.11 = (bf16[64,8,1024]{2,1,0:T(8,128)(2,1)}, bf16[64,8,1024]{2,1,0:T(8,128)(2,1)S(1)}, u32[]{:S(2)}, u32[]{:S(2)}) collective-permute-start(bf16[64,8,1024]{2,1,0:T(8,128)(2,1)} %get-tuple-element.59), channel_id=1, source_target_pairs={{0,1},{1,2},{2,3},{3,4},{4,5},{5,6},{6,7},{7,0},{8,9},{9,10},{10,1... | collective-permute-start | bytes 3145736 | tf_op jit(solution)/shard_map/ppermute | solution.py:454
  62.9 0.9 collective-permute-done.3
  63.9 1.6 %add_convert_fusion = bf16[256,2048]{1,0:T(8,128)(2,1)S(1)} fusion(bf16[256,2048]{1,0:T(8,128)(2,1)S(1)} %collective-permute-done.3, bf16[256,2048]{1,0:T(8,128)(2,1)} %get-tuple-element.40), kind=kLoop, calls=%fused_computation | loop fusion | flops 2097152 | bytes 3145728 | tf_op jit(solution)/shard_map/convert_element_type | solution.py:558
  65.5 0.1 dynamic-slice_bitcast_fusion
  65.7 0.2 collective-permute-start.5
  65.9 3.0 %collective-permute-start.6 = (bf16[2,32,2048]{2,1,0:T(8,128)(2,1)S(1)}, bf16[2,32,2048]{2,1,0:T(8,128)(2,1)S(1)}, u32[]{:S(2)}, u32[]{:S(2)}) collective-permute-start(bf16[2,32,2048]{2,1,0:T(8,128)(2,1)S(1)} %get-tuple-element.70), channel_id=1, source_target_pairs={{0,48},{16,0},{32,16},{48,32},{1,49},{17,1},{33,17},{49,33},{2,50}... | collective-permute-start | bytes 786440 | tf_op jit(solution)/shard_map/ppermute | solution.py:463
  68.9 1.0 collective-permute-start.7
  69.9 5.1 %shard_map.113 = (bf16[64,32,512]{2,1,0:T(8,128)(2,1)}, bf16[64,32,512]{2,1,0:T(8,128)(2,1)}) custom-call(s32[2]{0:T(128)} %shifts.7, bf16[64,32,512]{2,1,0:T(8,128)(2,1)} %get-tuple-element.44.updated, bf16[64,32,512]{2,1,0:T(8,128)(2,1)} %get-tuple-element.45.tokens_grad, ...), custom_call_target="tpu_custom_call", output_to_operand_aliasing={{0}: (1, {}), {1}: (2, {})} | custom-call | tf_op jit(solution)/shard_map/pallas_call | solution.py:516
  74.9 12.4 %collective-permute-done.7.in_cor = bf16[8,8,1024]{2,1,0:T(8,128)(2,1)S(1)} collective-permute-done((bf16[8,8,1024]{2,1,0:T(8,128)(2,1)}, bf16[8,8,1024]{2,1,0:T(8,128)(2,1)S(1)}, u32[]{:S(2)}, u32[]{:S(2)}) %collective-permute-start.7) | collective-permute-done | bytes 131104 | tf_op jit(solution)/shard_map/ppermute | solution.py:454
  87.3 4.2 %collective-permute-start.12 = (bf16[8,32,1024]{2,1,0:T(8,128)(2,1)}, bf16[8,32,1024]{2,1,0:T(8,128)(2,1)S(1)}, u32[]{:S(2)}, u32[]{:S(2)}) collective-permute-start(bf16[8,32,1024]{2,1,0:T(8,128)(2,1)} %get-tuple-element.60), channel_id=1, source_target_pairs={{0,8},{1,9},{2,10},{3,11},{4,12},{5,13},{6,14},{7,15},{8,16},{9,17... | collective-permute-start | bytes 1572872 | tf_op jit(solution)/shard_map/ppermute | solution.py:454
  91.5 0.1 fusion
  91.8 1.0 collective-permute-start.9
  92.8 2.2 %collective-permute-start.10 = (bf16[2,8,2048]{2,1,0:T(8,128)(2,1)S(1)}, bf16[2,8,2048]{2,1,0:T(8,128)(2,1)S(1)}, u32[]{:S(2)}, u32[]{:S(2)}) collective-permute-start(bf16[2,8,2048]{2,1,0:T(8,128)(2,1)S(1)} %get-tuple-element.74), channel_id=1, source_target_pairs={{0,6},{2,0},{4,2},{6,4},{1,7},{3,1},{5,3},{7,5},{8,14},{10,8},{12,... | collective-permute-start | bytes 196616 | tf_op jit(solution)/shard_map/ppermute | solution.py:463
  95.0 4.9 %collective-permute-done.12.in_lon = bf16[8,32,1024]{2,1,0:T(8,128)(2,1)S(1)} collective-permute-done((bf16[8,32,1024]{2,1,0:T(8,128)(2,1)}, bf16[8,32,1024]{2,1,0:T(8,128)(2,1)S(1)}, u32[]{:S(2)}, u32[]{:S(2)}) %collective-permute-start.12) | collective-permute-done | bytes 524320 | tf_op jit(solution)/shard_map/ppermute | solution.py:454
  100.1 0.4 collective-permute-start.15
  100.5 3.4 %collective-permute-start.14 = (bf16[4,2048]{1,0:T(4,128)(2,1)S(1)}, bf16[4,2048]{1,0:T(4,128)(2,1)S(1)}, u32[]{:S(2)}, u32[]{:S(2)}) collective-permute-start(bf16[4,2048]{1,0:T(4,128)(2,1)S(1)} %get-tuple-element.80), channel_id=1, source_target_pairs={{0,64},{1,65},{64,0},{65,1},{2,66},{3,67},{66,2},{67,3},{4,68},{5,... | collective-permute-start | bytes 49160 | tf_op jit(solution)/shard_map/ppermute | solution.py:463
  103.9 4.5 %shard_map.114 = (bf16[64,32,512]{2,1,0:T(8,128)(2,1)}, bf16[64,32,512]{2,1,0:T(8,128)(2,1)}) custom-call(s32[2]{0:T(128)} %shifts.7, bf16[64,32,512]{2,1,0:T(8,128)(2,1)} %get-tuple-element.53.updated, bf16[64,32,512]{2,1,0:T(8,128)(2,1)} %get-tuple-element.54.tokens_grad, ...), custom_call_target="tpu_custom_call", output_to_operand_aliasing={{0}: (1, {}), {1}: (2, {})} | custom-call | tf_op jit(solution)/shard_map/pallas_call | solution.py:527
  108.4 0.4 collective-permute-done.13
  108.9 0.6 slice.32
  109.5 0.6 slice.33
  (43 shorter events, 0.5 us)
Async XLA Ops:
  0.6 1.0 slice-start.2
  0.6 1.2 %slice-start = ((bf16[64,32,512]{2,1,0:T(8,128)(2,1)}), bf16[64,8,512]{2,1,0:T(8,128)(2,1)S(1)}, s32[]{:S(2)}) async-start(bf16[64,32,512]{2,1,0:T(8,128)(2,1)} %tokens_in.3), calls=%async_computation | async-start | bytes 1048576 | tf_op jit(solution)/shard_map/slice | solution.py:538
  0.7 5.9 %slice-start.1 = ((bf16[64,32,512]{2,1,0:T(8,128)(2,1)}), bf16[8,32,512]{2,1,0:T(8,128)(2,1)S(1)}, s32[]{:S(2)}) async-start(bf16[64,32,512]{2,1,0:T(8,128)(2,1)} %tokens_in.3), calls=%async_computation.1 | async-start | bytes 524288 | tf_op jit(solution)/shard_map/slice | solution.py:538
  0.7 5.8 %slice-start.3 = ((bf16[64,32,512]{2,1,0:T(8,128)(2,1)}), bf16[8,32,512]{2,1,0:T(8,128)(2,1)S(1)}, s32[]{:S(2)}) async-start(bf16[64,32,512]{2,1,0:T(8,128)(2,1)} %grads_in.3), calls=%async_computation.3 | async-start | bytes 524288 | tf_op jit(solution)/shard_map/slice | solution.py:538
  0.7 10.9 %copy-start.1 = (bf16[64,32,512]{2,1,0:T(8,128)(2,1)S(1)}, bf16[64,32,512]{2,1,0:T(8,128)(2,1)}, u32[]{:S(2)}) copy-start(bf16[64,32,512]{2,1,0:T(8,128)(2,1)} %grads_in.3) | copy-start | bytes 6291460
  1.8 9.8 %copy-start = (bf16[64,32,512]{2,1,0:T(8,128)(2,1)S(1)}, bf16[64,32,512]{2,1,0:T(8,128)(2,1)}, u32[]{:S(2)}) copy-start(bf16[64,32,512]{2,1,0:T(8,128)(2,1)} %tokens_in.3) | copy-start | bytes 6291460
  2.0 39.4 %collective-permute-start.1 = (bf16[64,8,1024]{2,1,0:T(8,128)(2,1)S(1)}, bf16[64,8,1024]{2,1,0:T(8,128)(2,1)S(1)}, u32[]{:S(2)}, u32[]{:S(2)}) collective-permute-start(bf16[64,8,1024]{2,1,0:T(8,128)(2,1)S(1)} %pad_maximum_fusion), channel_id=1, source_target_pairs={{0,7},{1,0},{2,1},{3,2},{4,3},{5,4},{6,5},{7,6},{8,15},{9,8},{10,9... | collective-permute-start | bytes 3145736 | tf_op jit(solution)/shard_map/ppermute | solution.py:454
  6.6 34.8 %collective-permute-start = (bf16[8,32,1024]{2,1,0:T(8,128)(2,1)S(1)}, bf16[8,32,1024]{2,1,0:T(8,128)(2,1)S(1)}, u32[]{:S(2)}, u32[]{:S(2)}) collective-permute-start(bf16[8,32,1024]{2,1,0:T(8,128)(2,1)S(1)} %pad_maximum_fusion.1), channel_id=1, source_target_pairs={{0,120},{1,121},{2,122},{3,123},{4,124},{5,125},{6,126},{7,127},{8... | collective-permute-start | bytes 1572872 | tf_op jit(solution)/shard_map/ppermute | solution.py:454
  11.6 29.7 %collective-permute-start.2 = (bf16[8,8,1024]{2,1,0:T(8,128)(2,1)S(1)}, bf16[8,8,1024]{2,1,0:T(8,128)(2,1)S(1)}, u32[]{:S(2)}, u32[]{:S(2)}) collective-permute-start(bf16[8,8,1024]{2,1,0:T(8,128)(2,1)S(1)} %pad_maximum_fusion.2), channel_id=1, source_target_pairs={{0,127},{1,120},{2,121},{3,122},{4,123},{5,124},{6,125},{7,126},{8... | collective-permute-start | bytes 393224 | tf_op jit(solution)/shard_map/ppermute | solution.py:454
  41.3 0.7 copy-start.6
  41.3 0.8 copy-start.5
  41.4 1.2 %copy-start.2 = (bf16[64,8,1024]{2,1,0:T(8,128)(2,1)}, bf16[64,8,1024]{2,1,0:T(8,128)(2,1)S(1)}, u32[]{:S(2)}) copy-start(bf16[64,8,1024]{2,1,0:T(8,128)(2,1)S(1)} %collective-permute-done.1.halo_lat) | copy-start | bytes 3145732
  60.9 3.0 %collective-permute-start.3 = (bf16[256,2048]{1,0:T(8,128)(2,1)}, bf16[256,2048]{1,0:T(8,128)(2,1)S(1)}, u32[]{:S(2)}, u32[]{:S(2)}) collective-permute-start(bf16[256,2048]{1,0:T(8,128)(2,1)} %get-tuple-element.41), channel_id=1, source_target_pairs={{0,8},{8,0},{1,9},{9,1},{2,10},{10,2},{3,11},{11,3},{4,12},{12,4},... | collective-permute-start | bytes 3145736 | tf_op jit(solution)/shard_map/ppermute | solution.py:554
  61.0 38.9 %collective-permute-start.11 = (bf16[64,8,1024]{2,1,0:T(8,128)(2,1)}, bf16[64,8,1024]{2,1,0:T(8,128)(2,1)S(1)}, u32[]{:S(2)}, u32[]{:S(2)}) collective-permute-start(bf16[64,8,1024]{2,1,0:T(8,128)(2,1)} %get-tuple-element.59), channel_id=1, source_target_pairs={{0,1},{1,2},{2,3},{3,4},{4,5},{5,6},{6,7},{7,0},{8,9},{9,10},{10,1... | collective-permute-start | bytes 3145736 | tf_op jit(solution)/shard_map/ppermute | solution.py:454
  65.6 25.9 %collective-permute-start.4 = (bf16[2,32,2048]{2,1,0:T(8,128)(2,1)S(1)}, bf16[2,32,2048]{2,1,0:T(8,128)(2,1)S(1)}, u32[]{:S(2)}, u32[]{:S(2)}) collective-permute-start(bf16[2,32,2048]{2,1,0:T(8,128)(2,1)S(1)} %get-tuple-element.72), channel_id=1, source_target_pairs={{0,16},{16,32},{32,48},{48,0},{1,17},{17,33},{33,49},{49,1},{2,18}... | collective-permute-start | bytes 786440 | tf_op jit(solution)/shard_map/ppermute | solution.py:463
  65.7 25.8 %collective-permute-start.5 = (bf16[2,32,2048]{2,1,0:T(8,128)(2,1)S(1)}, bf16[2,32,2048]{2,1,0:T(8,128)(2,1)S(1)}, u32[]{:S(2)}, u32[]{:S(2)}) collective-permute-start(bf16[2,32,2048]{2,1,0:T(8,128)(2,1)S(1)} %get-tuple-element.71), channel_id=1, source_target_pairs={{0,32},{16,48},{32,0},{48,16},{1,33},{17,49},{33,1},{49,17},{2,34}... | collective-permute-start | bytes 786440 | tf_op jit(solution)/shard_map/ppermute | solution.py:463
  65.9 25.6 %collective-permute-start.6 = (bf16[2,32,2048]{2,1,0:T(8,128)(2,1)S(1)}, bf16[2,32,2048]{2,1,0:T(8,128)(2,1)S(1)}, u32[]{:S(2)}, u32[]{:S(2)}) collective-permute-start(bf16[2,32,2048]{2,1,0:T(8,128)(2,1)S(1)} %get-tuple-element.70), channel_id=1, source_target_pairs={{0,48},{16,0},{32,16},{48,32},{1,49},{17,1},{33,17},{49,33},{2,50}... | collective-permute-start | bytes 786440 | tf_op jit(solution)/shard_map/ppermute | solution.py:463
  68.9 18.4 %collective-permute-start.7 = (bf16[8,8,1024]{2,1,0:T(8,128)(2,1)}, bf16[8,8,1024]{2,1,0:T(8,128)(2,1)S(1)}, u32[]{:S(2)}, u32[]{:S(2)}) collective-permute-start(bf16[8,8,1024]{2,1,0:T(8,128)(2,1)} %get-tuple-element.52), channel_id=1, source_target_pairs={{0,9},{1,10},{2,11},{3,12},{4,13},{5,14},{6,15},{7,8},{8,17},{9,18... | collective-permute-start | bytes 393224 | tf_op jit(solution)/shard_map/ppermute | solution.py:454
  87.3 16.6 %copy-start.7 = (bf16[8,8,1024]{2,1,0:T(8,128)(2,1)}, bf16[8,8,1024]{2,1,0:T(8,128)(2,1)S(1)}, u32[]{:S(2)}) copy-start(bf16[8,8,1024]{2,1,0:T(8,128)(2,1)S(1)} %collective-permute-done.7.in_cor) | copy-start | bytes 393220
  87.3 12.6 %collective-permute-start.12 = (bf16[8,32,1024]{2,1,0:T(8,128)(2,1)}, bf16[8,32,1024]{2,1,0:T(8,128)(2,1)S(1)}, u32[]{:S(2)}, u32[]{:S(2)}) collective-permute-start(bf16[8,32,1024]{2,1,0:T(8,128)(2,1)} %get-tuple-element.60), channel_id=1, source_target_pairs={{0,8},{1,9},{2,10},{3,11},{4,12},{5,13},{6,14},{7,15},{8,16},{9,17... | collective-permute-start | bytes 1572872 | tf_op jit(solution)/shard_map/ppermute | solution.py:454
  91.7 8.3 %collective-permute-start.8 = (bf16[2,8,2048]{2,1,0:T(8,128)(2,1)S(1)}, bf16[2,8,2048]{2,1,0:T(8,128)(2,1)S(1)}, u32[]{:S(2)}, u32[]{:S(2)}) collective-permute-start(bf16[2,8,2048]{2,1,0:T(8,128)(2,1)S(1)} %get-tuple-element.76), channel_id=1, source_target_pairs={{0,2},{2,4},{4,6},{6,0},{1,3},{3,5},{5,7},{7,1},{8,10},{10,12},{12... | collective-permute-start | bytes 196616 | tf_op jit(solution)/shard_map/ppermute | solution.py:463
  91.8 8.2 %collective-permute-start.9 = (bf16[2,8,2048]{2,1,0:T(8,128)(2,1)S(1)}, bf16[2,8,2048]{2,1,0:T(8,128)(2,1)S(1)}, u32[]{:S(2)}, u32[]{:S(2)}) collective-permute-start(bf16[2,8,2048]{2,1,0:T(8,128)(2,1)S(1)} %get-tuple-element.75), channel_id=1, source_target_pairs={{0,4},{2,6},{4,0},{6,2},{1,5},{3,7},{5,1},{7,3},{8,12},{10,14},{12... | collective-permute-start | bytes 196616 | tf_op jit(solution)/shard_map/ppermute | solution.py:463
  92.8 7.2 %collective-permute-start.10 = (bf16[2,8,2048]{2,1,0:T(8,128)(2,1)S(1)}, bf16[2,8,2048]{2,1,0:T(8,128)(2,1)S(1)}, u32[]{:S(2)}, u32[]{:S(2)}) collective-permute-start(bf16[2,8,2048]{2,1,0:T(8,128)(2,1)S(1)} %get-tuple-element.74), channel_id=1, source_target_pairs={{0,6},{2,0},{4,2},{6,4},{1,7},{3,1},{5,3},{7,5},{8,14},{10,8},{12,... | collective-permute-start | bytes 196616 | tf_op jit(solution)/shard_map/ppermute | solution.py:463
  100.0 4.0 %copy-start.4 = (bf16[8,32,1024]{2,1,0:T(8,128)(2,1)}, bf16[8,32,1024]{2,1,0:T(8,128)(2,1)S(1)}, u32[]{:S(2)}) copy-start(bf16[8,32,1024]{2,1,0:T(8,128)(2,1)S(1)} %collective-permute-done.12.in_lon) | copy-start | bytes 1572868
  100.0 4.0 %copy-start.3 = (bf16[64,8,1024]{2,1,0:T(8,128)(2,1)}, bf16[64,8,1024]{2,1,0:T(8,128)(2,1)S(1)}, u32[]{:S(2)}) copy-start(bf16[64,8,1024]{2,1,0:T(8,128)(2,1)S(1)} %collective-permute-done.11.in_lat) | copy-start | bytes 3145732
  100.1 8.3 %collective-permute-start.15 = (bf16[4,2048]{1,0:T(4,128)(2,1)S(1)}, bf16[4,2048]{1,0:T(4,128)(2,1)S(1)}, u32[]{:S(2)}, u32[]{:S(2)}) collective-permute-start(bf16[4,2048]{1,0:T(4,128)(2,1)S(1)} %get-tuple-element.79), channel_id=1, source_target_pairs={{0,65},{1,0},{64,1},{65,64},{2,67},{3,2},{66,3},{67,66},{4,69},{5,... | collective-permute-start | bytes 49160 | tf_op jit(solution)/shard_map/ppermute | solution.py:463
  100.5 7.9 %collective-permute-start.14 = (bf16[4,2048]{1,0:T(4,128)(2,1)S(1)}, bf16[4,2048]{1,0:T(4,128)(2,1)S(1)}, u32[]{:S(2)}, u32[]{:S(2)}) collective-permute-start(bf16[4,2048]{1,0:T(4,128)(2,1)S(1)} %get-tuple-element.80), channel_id=1, source_target_pairs={{0,64},{1,65},{64,0},{65,1},{2,66},{3,67},{66,2},{67,3},{4,68},{5,... | collective-permute-start | bytes 49160 | tf_op jit(solution)/shard_map/ppermute | solution.py:463
  103.9 4.9 %collective-permute-start.13 = (bf16[4,2048]{1,0:T(4,128)(2,1)S(1)}, bf16[4,2048]{1,0:T(4,128)(2,1)S(1)}, u32[]{:S(2)}, u32[]{:S(2)}) collective-permute-start(bf16[4,2048]{1,0:T(4,128)(2,1)S(1)} %get-tuple-element.78), channel_id=1, source_target_pairs={{0,1},{1,64},{64,65},{65,0},{2,3},{3,66},{66,67},{67,2},{4,5},{5,6... | collective-permute-start | bytes 49160 | tf_op jit(solution)/shard_map/ppermute | solution.py:463

commit v4 on v3

--- a/solution.py
+++ b/solution.py
@@ -549,7 +549,7 @@
 
     def merge_beside(blocks):
         _, *placed = lax.optimization_barrier((blocks, updated, tokens_grad))
-        return *run_edge_merge(shifts, *placed, *edges), in_cor
+        return run_edge_merge(shifts, *placed, *edges)
 
     w_got = lax.ppermute(w_other, "core", [(0, 1), (1, 0)])
     in_lat = shift_to(out_lat, 0, 1)
@@ -557,7 +557,7 @@
     in_cor = shift_to(out_cor, 1, 1)
     total = (w_mine.astype(F32) + w_got.astype(F32)).astype(BF)
     total = total.reshape(2, 4, 32, 4 * D).transpose(1, 0, 2, 3)
-    total, (updated, tokens_grad, in_cor) = scatter_sum(total, "x", 4, merge_beside)
+    total, (updated, tokens_grad) = scatter_sum(total, "x", 4, merge_beside)
     total = total.astype(BF).reshape(2, 4, 8, 4 * D).transpose(1, 0, 2, 3)
     total, (in_lat, in_lon) = scatter_sum(total, "y", 4, lambda blocks: (in_lat, in_lon))
     total, _ = scatter_sum(total.astype(BF).reshape(4, 4, 4 * D), ("zh", "zl"), 4)

time: 110 us -> 107 us (0.973)
  starting transfers between devices: 27.3 us -> 24.2 us
    ppermute x6, waiting for transfers between devices: 17.4 us -> 9.33 us  [shift_to(): return lax.ppermute(value, ALL, pairs)]
    ppermute x9, waiting for transfers between devices: 0.47 us -> 7.65 us  [scatter_sum(): parts.append(lax.ppermute(block, axes, pairs))]
    ppermute x6, starting transfers between devices: 16.8 us -> 11.7 us  [shift_to(): return lax.ppermute(value, ALL, pairs)]
    ppermute x9, starting transfers between devices: 10.4 us -> 12.4 us  [scatter_sum(): parts.append(lax.ppermute(block, axes, pairs))]
  transfers between devices with their start and end apart: 16 -> 16, of which waited for: 4 -> 4; matrix products, arithmetic and copies ran while one was open for 2% -> 2% of each run, Pallas kernels for 35% -> 36%
where the time goes in v4:
time: 107 us
  Pallas kernels  57.3 us (54%)
  starting transfers between devices  24.2 us (23%)
  waiting for transfers between devices  17.9 us (17%)
  local copies, waits for them, and re-layouts  4.41 us (4%)
  other arithmetic  2.01 us (2%)
    pallas_call x1, Pallas kernels, run_interior(): call(interior_kernel, [GRID, GRID, sds((D, 4 * D), F32), sds((32, 128), F...  29.4 us
    pallas_call x1, Pallas kernels, run_edge(): call(edge_kernel, [sds(shape, BF) for shape in (lat, lon, lat, lon, far_l...  18.4 us
    ppermute x9, starting transfers between devices, scatter_sum(): parts.append(lax.ppermute(block, axes, pairs))  12.4 us
    ppermute x6, starting transfers between devices, shift_to(): return lax.ppermute(value, ALL, pairs)  11.7 us
    ppermute x6, waiting for transfers between devices, shift_to(): return lax.ppermute(value, ALL, pairs)  9.33 us
    ppermute x9, waiting for transfers between devices, scatter_sum(): parts.append(lax.ppermute(block, axes, pairs))  7.65 us
    pallas_call x1, Pallas kernels, run_edge_merge(): call(edge_merge_kernel, [GRID, GRID], [vmem((2, 64, 16, D), BF), vmem((2,...  5.1 us
    pallas_call x1, Pallas kernels, run_return(): call(return_kernel, [GRID, GRID], [vmem((2, 64, 16, D), BF), vmem((2, 8,...  4.45 us
  transfers between devices with their start and end apart: 16, of which 4 were waited for; matrix products, arithmetic and copies ran while one was open for 2% of the time, Pallas kernels for 36%

profile of v4, /device:TPU:0, one launch (start us, length us, event | category | flops | bytes accessed | tf_op | source)
XLA Modules:
  0.0 106.8 jit_solution(5204453104328847481)
XLA Ops:
  0.7 1.0 slice-done.2
  1.7 0.2 slice-done
  1.8 0.1 pad_maximum_fusion
  2.0 4.5 %collective-permute-start.1 = (bf16[64,8,1024]{2,1,0:T(8,128)(2,1)S(1)}, bf16[64,8,1024]{2,1,0:T(8,128)(2,1)S(1)}, u32[]{:S(2)}, u32[]{:S(2)}) collective-permute-start(bf16[64,8,1024]{2,1,0:T(8,128)(2,1)S(1)} %pad_maximum_fusion), channel_id=1, source_target_pairs={{0,7},{1,0},{2,1},{3,2},{4,3},{5,4},{6,5},{7,6},{8,15},{9,8},{10,9... | collective-permute-start | bytes 3145736 | tf_op jit(solution)/shard_map/ppermute | solution.py:454
  6.6 5.0 %collective-permute-start = (bf16[8,32,1024]{2,1,0:T(8,128)(2,1)S(1)}, bf16[8,32,1024]{2,1,0:T(8,128)(2,1)S(1)}, u32[]{:S(2)}, u32[]{:S(2)}) collective-permute-start(bf16[8,32,1024]{2,1,0:T(8,128)(2,1)S(1)} %pad_maximum_fusion.1), channel_id=1, source_target_pairs={{0,120},{1,121},{2,122},{3,123},{4,124},{5,125},{6,126},{7,127},{8... | collective-permute-start | bytes 1572872 | tf_op jit(solution)/shard_map/ppermute | solution.py:454
  11.6 0.3 collective-permute-start.2
  11.9 29.4 %shard_map.111 = (bf16[64,32,512]{2,1,0:T(8,128)(2,1)}, bf16[64,32,512]{2,1,0:T(8,128)(2,1)}, f32[512,2048]{1,0:T(8,128)}, f32[32,128]{1,0:T(8,128)}, f32[64,512]{1,0:T(8,128)}) custom-call(s32[2]{0:T(128)} %shifts.7, bf16[64,32,512]{2,1,0:T(8,128)(2,1)} %tokens_in.3, bf16[64,32,512]{2,1,0:T(8,128)(2,1)} %grads_in.3, s32[1024,256]{1,0:T(8,128)} %pad_in.1, ...), custom_call_target="tpu_custom_call" | custom-call | tf_op jit(solution)/shard_map/pallas_call | solution.py:484
  41.4 0.6 copy-done.6
  42.0 0.2 copy-done.5
  42.2 0.3 copy-done.2
  42.5 18.4 %shard_map.112 = (bf16[64,16,512]{2,1,0:T(8,128)(2,1)}, bf16[8,32,512]{2,1,0:T(8,128)(2,1)}, bf16[64,16,512]{2,1,0:T(8,128)(2,1)}, bf16[8,32,512]{2,1,0:T(8,128)...) custom-call(s32[2]{0:T(128)} %shifts.7, ...), custom_call_target="tpu_custom_call" | custom-call | tf_op jit(solution)/shard_map/pallas_call | solution.py:499
  60.9 0.1 collective-permute-start.3
  61.0 1.9 %collective-permute-start.10 = (bf16[64,8,1024]{2,1,0:T(8,128)(2,1)}, bf16[64,8,1024]{2,1,0:T(8,128)(2,1)S(1)}, u32[]{:S(2)}, u32[]{:S(2)}) collective-permute-start(bf16[64,8,1024]{2,1,0:T(8,128)(2,1)} %get-tuple-element.57), channel_id=1, source_target_pairs={{0,1},{1,2},{2,3},{3,4},{4,5},{5,6},{6,7},{7,0},{8,9},{9,10},{10,1... | collective-permute-start | bytes 3145736 | tf_op jit(solution)/shard_map/ppermute | solution.py:454
  62.9 0.9 collective-permute-done.3
  63.8 1.6 %add_convert_fusion = bf16[256,2048]{1,0:T(8,128)(2,1)S(1)} fusion(bf16[256,2048]{1,0:T(8,128)(2,1)S(1)} %collective-permute-done.3, bf16[256,2048]{1,0:T(8,128)(2,1)} %get-tuple-element.39), kind=kLoop, calls=%fused_computation | loop fusion | flops 2097152 | bytes 3145728 | tf_op jit(solution)/shard_map/convert_element_type | solution.py:558
  65.4 0.1 dynamic-slice_bitcast_fusion
  65.6 0.1 collective-permute-start.4
  65.6 0.2 collective-permute-start.5
  65.9 3.0 %collective-permute-start.6 = (bf16[2,32,2048]{2,1,0:T(8,128)(2,1)S(1)}, bf16[2,32,2048]{2,1,0:T(8,128)(2,1)S(1)}, u32[]{:S(2)}, u32[]{:S(2)}) collective-permute-start(bf16[2,32,2048]{2,1,0:T(8,128)(2,1)S(1)} %get-tuple-element.68), channel_id=1, source_target_pairs={{0,48},{16,0},{32,16},{48,32},{1,49},{17,1},{33,17},{49,33},{2,50}... | collective-permute-start | bytes 786440 | tf_op jit(solution)/shard_map/ppermute | solution.py:463
  68.9 5.1 %shard_map.113 = (bf16[64,32,512]{2,1,0:T(8,128)(2,1)}, bf16[64,32,512]{2,1,0:T(8,128)(2,1)}) custom-call(s32[2]{0:T(128)} %shifts.7, bf16[64,32,512]{2,1,0:T(8,128)(2,1)} %get-tuple-element.43.updated, bf16[64,32,512]{2,1,0:T(8,128)(2,1)} %get-tuple-element.44.tokens_grad, ...), custom_call_target="tpu_custom_call", output_to_operand_aliasing={{0}: (1, {}), {1}: (2, {})} | custom-call | tf_op jit(solution)/shard_map/pallas_call | solution.py:516
  74.0 7.6 %collective-permute-done.4 = bf16[2,32,2048]{2,1,0:T(8,128)(2,1)S(1)} collective-permute-done((bf16[2,32,2048]{2,1,0:T(8,128)(2,1)S(1)}, bf16[2,32,2048]{2,1,0:T(8,128)(2,1)S(1)}, u32[]{:S(2)}, u32[]{:S(2)}) %collective-permute-start.4) | collective-permute-done | bytes 262176 | tf_op jit(solution)/shard_map/ppermute | solution.py:463
  81.6 0.1 fusion
  81.9 2.2 %collective-permute-start.8 = (bf16[2,8,2048]{2,1,0:T(8,128)(2,1)S(1)}, bf16[2,8,2048]{2,1,0:T(8,128)(2,1)S(1)}, u32[]{:S(2)}, u32[]{:S(2)}) collective-permute-start(bf16[2,8,2048]{2,1,0:T(8,128)(2,1)S(1)} %get-tuple-element.73), channel_id=1, source_target_pairs={{0,4},{2,6},{4,0},{6,2},{1,5},{3,7},{5,1},{7,3},{8,12},{10,14},{12... | collective-permute-start | bytes 196616 | tf_op jit(solution)/shard_map/ppermute | solution.py:463
  84.1 1.1 collective-permute-start.9
  85.1 1.5 %collective-permute-done.11.in_lon = bf16[8,32,1024]{2,1,0:T(8,128)(2,1)S(1)} collective-permute-done((bf16[8,32,1024]{2,1,0:T(8,128)(2,1)}, bf16[8,32,1024]{2,1,0:T(8,128)(2,1)S(1)}, u32[]{:S(2)}, u32[]{:S(2)}) %collective-permute-start.11) | collective-permute-done | bytes 524320 | tf_op jit(solution)/shard_map/ppermute | solution.py:454
  86.6 7.8 %collective-permute-done.10.in_lat = bf16[64,8,1024]{2,1,0:T(8,128)(2,1)S(1)} collective-permute-done((bf16[64,8,1024]{2,1,0:T(8,128)(2,1)}, bf16[64,8,1024]{2,1,0:T(8,128)(2,1)S(1)}, u32[]{:S(2)}, u32[]{:S(2)}) %collective-permute-start.10) | collective-permute-done | bytes 1048608 | tf_op jit(solution)/shard_map/ppermute | solution.py:454
  94.6 2.9 %collective-permute-start.15 = (bf16[4,2048]{1,0:T(4,128)(2,1)S(1)}, bf16[4,2048]{1,0:T(4,128)(2,1)S(1)}, u32[]{:S(2)}, u32[]{:S(2)}) collective-permute-start(bf16[4,2048]{1,0:T(4,128)(2,1)S(1)} %get-tuple-element.77), channel_id=1, source_target_pairs={{0,65},{1,0},{64,1},{65,64},{2,67},{3,2},{66,3},{67,66},{4,69},{5,... | collective-permute-start | bytes 49160 | tf_op jit(solution)/shard_map/ppermute | solution.py:463
  97.5 2.9 %collective-permute-start.14 = (bf16[4,2048]{1,0:T(4,128)(2,1)S(1)}, bf16[4,2048]{1,0:T(4,128)(2,1)S(1)}, u32[]{:S(2)}, u32[]{:S(2)}) collective-permute-start(bf16[4,2048]{1,0:T(4,128)(2,1)S(1)} %get-tuple-element.78), channel_id=1, source_target_pairs={{0,64},{1,65},{64,0},{65,1},{2,66},{3,67},{66,2},{67,3},{4,68},{5,... | collective-permute-start | bytes 49160 | tf_op jit(solution)/shard_map/ppermute | solution.py:463
  100.4 0.6 copy-done.7
  101.1 4.4 %shard_map.114 = (bf16[64,32,512]{2,1,0:T(8,128)(2,1)}, bf16[64,32,512]{2,1,0:T(8,128)(2,1)}) custom-call(s32[2]{0:T(128)} %shifts.7, bf16[64,32,512]{2,1,0:T(8,128)(2,1)} %get-tuple-element.51.updated, bf16[64,32,512]{2,1,0:T(8,128)(2,1)} %get-tuple-element.52.tokens_grad, ...), custom_call_target="tpu_custom_call", output_to_operand_aliasing={{0}: (1, {}), {1}: (2, {})} | custom-call | tf_op jit(solution)/shard_map/pallas_call | solution.py:527
  105.6 0.6 slice.32
  106.2 0.6 slice.33
  (45 shorter events, 0.4 us)
Async XLA Ops:
  0.6 1.0 slice-start.2
  0.6 1.2 %slice-start = ((bf16[64,32,512]{2,1,0:T(8,128)(2,1)}), bf16[64,8,512]{2,1,0:T(8,128)(2,1)S(1)}, s32[]{:S(2)}) async-start(bf16[64,32,512]{2,1,0:T(8,128)(2,1)} %tokens_in.3), calls=%async_computation | async-start | bytes 1048576 | tf_op jit(solution)/shard_map/slice | solution.py:538
  0.7 5.9 %slice-start.1 = ((bf16[64,32,512]{2,1,0:T(8,128)(2,1)}), bf16[8,32,512]{2,1,0:T(8,128)(2,1)S(1)}, s32[]{:S(2)}) async-start(bf16[64,32,512]{2,1,0:T(8,128)(2,1)} %tokens_in.3), calls=%async_computation.1 | async-start | bytes 524288 | tf_op jit(solution)/shard_map/slice | solution.py:538
  0.7 5.8 %slice-start.3 = ((bf16[64,32,512]{2,1,0:T(8,128)(2,1)}), bf16[8,32,512]{2,1,0:T(8,128)(2,1)S(1)}, s32[]{:S(2)}) async-start(bf16[64,32,512]{2,1,0:T(8,128)(2,1)} %grads_in.3), calls=%async_computation.3 | async-start | bytes 524288 | tf_op jit(solution)/shard_map/slice | solution.py:538
  0.7 10.9 %copy-start.1 = (bf16[64,32,512]{2,1,0:T(8,128)(2,1)S(1)}, bf16[64,32,512]{2,1,0:T(8,128)(2,1)}, u32[]{:S(2)}) copy-start(bf16[64,32,512]{2,1,0:T(8,128)(2,1)} %grads_in.3) | copy-start | bytes 6291460
  1.8 9.8 %copy-start = (bf16[64,32,512]{2,1,0:T(8,128)(2,1)S(1)}, bf16[64,32,512]{2,1,0:T(8,128)(2,1)}, u32[]{:S(2)}) copy-start(bf16[64,32,512]{2,1,0:T(8,128)(2,1)} %tokens_in.3) | copy-start | bytes 6291460
  2.0 39.3 %collective-permute-start.1 = (bf16[64,8,1024]{2,1,0:T(8,128)(2,1)S(1)}, bf16[64,8,1024]{2,1,0:T(8,128)(2,1)S(1)}, u32[]{:S(2)}, u32[]{:S(2)}) collective-permute-start(bf16[64,8,1024]{2,1,0:T(8,128)(2,1)S(1)} %pad_maximum_fusion), channel_id=1, source_target_pairs={{0,7},{1,0},{2,1},{3,2},{4,3},{5,4},{6,5},{7,6},{8,15},{9,8},{10,9... | collective-permute-start | bytes 3145736 | tf_op jit(solution)/shard_map/ppermute | solution.py:454
  6.6 34.7 %collective-permute-start = (bf16[8,32,1024]{2,1,0:T(8,128)(2,1)S(1)}, bf16[8,32,1024]{2,1,0:T(8,128)(2,1)S(1)}, u32[]{:S(2)}, u32[]{:S(2)}) collective-permute-start(bf16[8,32,1024]{2,1,0:T(8,128)(2,1)S(1)} %pad_maximum_fusion.1), channel_id=1, source_target_pairs={{0,120},{1,121},{2,122},{3,123},{4,124},{5,125},{6,126},{7,127},{8... | collective-permute-start | bytes 1572872 | tf_op jit(solution)/shard_map/ppermute | solution.py:454
  11.6 29.7 %collective-permute-start.2 = (bf16[8,8,1024]{2,1,0:T(8,128)(2,1)S(1)}, bf16[8,8,1024]{2,1,0:T(8,128)(2,1)S(1)}, u32[]{:S(2)}, u32[]{:S(2)}) collective-permute-start(bf16[8,8,1024]{2,1,0:T(8,128)(2,1)S(1)} %pad_maximum_fusion.2), channel_id=1, source_target_pairs={{0,127},{1,120},{2,121},{3,122},{4,123},{5,124},{6,125},{7,126},{8... | collective-permute-start | bytes 393224 | tf_op jit(solution)/shard_map/ppermute | solution.py:454
  41.3 0.7 copy-start.6
  41.3 0.9 copy-start.5
  41.3 1.2 %copy-start.2 = (bf16[64,8,1024]{2,1,0:T(8,128)(2,1)}, bf16[64,8,1024]{2,1,0:T(8,128)(2,1)S(1)}, u32[]{:S(2)}) copy-start(bf16[64,8,1024]{2,1,0:T(8,128)(2,1)S(1)} %collective-permute-done.1.halo_lat) | copy-start | bytes 3145732
  60.9 3.0 %collective-permute-start.3 = (bf16[256,2048]{1,0:T(8,128)(2,1)}, bf16[256,2048]{1,0:T(8,128)(2,1)S(1)}, u32[]{:S(2)}, u32[]{:S(2)}) collective-permute-start(bf16[256,2048]{1,0:T(8,128)(2,1)} %get-tuple-element.40), channel_id=1, source_target_pairs={{0,8},{8,0},{1,9},{9,1},{2,10},{10,2},{3,11},{11,3},{4,12},{12,4},... | collective-permute-start | bytes 3145736 | tf_op jit(solution)/shard_map/ppermute | solution.py:554
  61.0 33.5 %collective-permute-start.10 = (bf16[64,8,1024]{2,1,0:T(8,128)(2,1)}, bf16[64,8,1024]{2,1,0:T(8,128)(2,1)S(1)}, u32[]{:S(2)}, u32[]{:S(2)}) collective-permute-start(bf16[64,8,1024]{2,1,0:T(8,128)(2,1)} %get-tuple-element.57), channel_id=1, source_target_pairs={{0,1},{1,2},{2,3},{3,4},{4,5},{5,6},{6,7},{7,0},{8,9},{9,10},{10,1... | collective-permute-start | bytes 3145736 | tf_op jit(solution)/shard_map/ppermute | solution.py:454
  65.6 16.0 %collective-permute-start.4 = (bf16[2,32,2048]{2,1,0:T(8,128)(2,1)S(1)}, bf16[2,32,2048]{2,1,0:T(8,128)(2,1)S(1)}, u32[]{:S(2)}, u32[]{:S(2)}) collective-permute-start(bf16[2,32,2048]{2,1,0:T(8,128)(2,1)S(1)} %get-tuple-element.70), channel_id=1, source_target_pairs={{0,16},{16,32},{32,48},{48,0},{1,17},{17,33},{33,49},{49,1},{2,18}... | collective-permute-start | bytes 786440 | tf_op jit(solution)/shard_map/ppermute | solution.py:463
  65.6 16.0 %collective-permute-start.5 = (bf16[2,32,2048]{2,1,0:T(8,128)(2,1)S(1)}, bf16[2,32,2048]{2,1,0:T(8,128)(2,1)S(1)}, u32[]{:S(2)}, u32[]{:S(2)}) collective-permute-start(bf16[2,32,2048]{2,1,0:T(8,128)(2,1)S(1)} %get-tuple-element.69), channel_id=1, source_target_pairs={{0,32},{16,48},{32,0},{48,16},{1,33},{17,49},{33,1},{49,17},{2,34}... | collective-permute-start | bytes 786440 | tf_op jit(solution)/shard_map/ppermute | solution.py:463
  65.9 15.8 %collective-permute-start.6 = (bf16[2,32,2048]{2,1,0:T(8,128)(2,1)S(1)}, bf16[2,32,2048]{2,1,0:T(8,128)(2,1)S(1)}, u32[]{:S(2)}, u32[]{:S(2)}) collective-permute-start(bf16[2,32,2048]{2,1,0:T(8,128)(2,1)S(1)} %get-tuple-element.68), channel_id=1, source_target_pairs={{0,48},{16,0},{32,16},{48,32},{1,49},{17,1},{33,17},{49,33},{2,50}... | collective-permute-start | bytes 786440 | tf_op jit(solution)/shard_map/ppermute | solution.py:463
  68.9 17.7 %collective-permute-start.11 = (bf16[8,32,1024]{2,1,0:T(8,128)(2,1)}, bf16[8,32,1024]{2,1,0:T(8,128)(2,1)S(1)}, u32[]{:S(2)}, u32[]{:S(2)}) collective-permute-start(bf16[8,32,1024]{2,1,0:T(8,128)(2,1)} %get-tuple-element.58), channel_id=1, source_target_pairs={{0,8},{1,9},{2,10},{3,11},{4,12},{5,13},{6,14},{7,15},{8,16},{9,17... | collective-permute-start | bytes 1572872 | tf_op jit(solution)/shard_map/ppermute | solution.py:454
  68.9 17.7 %copy-start.8 = (bf16[8,8,1024]{2,1,0:T(8,128)(2,1)S(1)}, bf16[8,8,1024]{2,1,0:T(8,128)(2,1)}, u32[]{:S(2)}) copy-start(bf16[8,8,1024]{2,1,0:T(8,128)(2,1)} %get-tuple-element.61) | copy-start | bytes 393220
  81.8 12.7 %collective-permute-start.7 = (bf16[2,8,2048]{2,1,0:T(8,128)(2,1)S(1)}, bf16[2,8,2048]{2,1,0:T(8,128)(2,1)S(1)}, u32[]{:S(2)}, u32[]{:S(2)}) collective-permute-start(bf16[2,8,2048]{2,1,0:T(8,128)(2,1)S(1)} %get-tuple-element.74), channel_id=1, source_target_pairs={{0,2},{2,4},{4,6},{6,0},{1,3},{3,5},{5,7},{7,1},{8,10},{10,12},{12... | collective-permute-start | bytes 196616 | tf_op jit(solution)/shard_map/ppermute | solution.py:463
  81.9 12.6 %collective-permute-start.8 = (bf16[2,8,2048]{2,1,0:T(8,128)(2,1)S(1)}, bf16[2,8,2048]{2,1,0:T(8,128)(2,1)S(1)}, u32[]{:S(2)}, u32[]{:S(2)}) collective-permute-start(bf16[2,8,2048]{2,1,0:T(8,128)(2,1)S(1)} %get-tuple-element.73), channel_id=1, source_target_pairs={{0,4},{2,6},{4,0},{6,2},{1,5},{3,7},{5,1},{7,3},{8,12},{10,14},{12... | collective-permute-start | bytes 196616 | tf_op jit(solution)/shard_map/ppermute | solution.py:463
  84.1 10.4 %collective-permute-start.9 = (bf16[2,8,2048]{2,1,0:T(8,128)(2,1)S(1)}, bf16[2,8,2048]{2,1,0:T(8,128)(2,1)S(1)}, u32[]{:S(2)}, u32[]{:S(2)}) collective-permute-start(bf16[2,8,2048]{2,1,0:T(8,128)(2,1)S(1)} %get-tuple-element.72), channel_id=1, source_target_pairs={{0,6},{2,0},{4,2},{6,4},{1,7},{3,1},{5,3},{7,5},{8,14},{10,8},{12,... | collective-permute-start | bytes 196616 | tf_op jit(solution)/shard_map/ppermute | solution.py:463
  86.6 13.8 %copy-start.4 = (bf16[8,32,1024]{2,1,0:T(8,128)(2,1)}, bf16[8,32,1024]{2,1,0:T(8,128)(2,1)S(1)}, u32[]{:S(2)}) copy-start(bf16[8,32,1024]{2,1,0:T(8,128)(2,1)S(1)} %collective-permute-done.11.in_lon) | copy-start | bytes 1572868
  86.6 13.8 %collective-permute-start.12 = (bf16[8,8,1024]{2,1,0:T(8,128)(2,1)S(1)}, bf16[8,8,1024]{2,1,0:T(8,128)(2,1)S(1)}, u32[]{:S(2)}, u32[]{:S(2)}) collective-permute-start(bf16[8,8,1024]{2,1,0:T(8,128)(2,1)S(1)} %copy-done.8), channel_id=1, source_target_pairs={{0,9},{1,10},{2,11},{3,12},{4,13},{5,14},{6,15},{7,8},{8,17},{9,18... | collective-permute-start | bytes 393224 | tf_op jit(solution)/shard_map/ppermute | solution.py:454
  94.5 6.0 %copy-start.3 = (bf16[64,8,1024]{2,1,0:T(8,128)(2,1)}, bf16[64,8,1024]{2,1,0:T(8,128)(2,1)S(1)}, u32[]{:S(2)}) copy-start(bf16[64,8,1024]{2,1,0:T(8,128)(2,1)S(1)} %collective-permute-done.10.in_lat) | copy-start | bytes 3145732
  94.6 10.9 %collective-permute-start.15 = (bf16[4,2048]{1,0:T(4,128)(2,1)S(1)}, bf16[4,2048]{1,0:T(4,128)(2,1)S(1)}, u32[]{:S(2)}, u32[]{:S(2)}) collective-permute-start(bf16[4,2048]{1,0:T(4,128)(2,1)S(1)} %get-tuple-element.77), channel_id=1, source_target_pairs={{0,65},{1,0},{64,1},{65,64},{2,67},{3,2},{66,3},{67,66},{4,69},{5,... | collective-permute-start | bytes 49160 | tf_op jit(solution)/shard_map/ppermute | solution.py:463
  97.5 8.0 %collective-permute-start.14 = (bf16[4,2048]{1,0:T(4,128)(2,1)S(1)}, bf16[4,2048]{1,0:T(4,128)(2,1)S(1)}, u32[]{:S(2)}, u32[]{:S(2)}) collective-permute-start(bf16[4,2048]{1,0:T(4,128)(2,1)S(1)} %get-tuple-element.78), channel_id=1, source_target_pairs={{0,64},{1,65},{64,0},{65,1},{2,66},{3,67},{66,2},{67,3},{4,68},{5,... | collective-permute-start | bytes 49160 | tf_op jit(solution)/shard_map/ppermute | solution.py:463
  100.4 5.1 %collective-permute-start.13 = (bf16[4,2048]{1,0:T(4,128)(2,1)S(1)}, bf16[4,2048]{1,0:T(4,128)(2,1)S(1)}, u32[]{:S(2)}, u32[]{:S(2)}) collective-permute-start(bf16[4,2048]{1,0:T(4,128)(2,1)S(1)} %get-tuple-element.76), channel_id=1, source_target_pairs={{0,1},{1,64},{64,65},{65,0},{2,3},{3,66},{66,67},{67,2},{4,5},{5,6... | collective-permute-start | bytes 49160 | tf_op jit(solution)/shard_map/ppermute | solution.py:463
  100.4 0.6 copy-start.7
